TPU v7x, 512 devices: a whole 4x8x8 slice. The times are simulated.
512 devices in a mesh: up: 32 (over y, x), lo: 16 (over z, core).
Axes of the slice: x: 4, y: 8, z: 8, core: 2. Of those that a mesh axis runs over, the one named last changes fastest.
Arguments:
- sector_sizes: int32 [8], replicated, may hold values from 1 to 384, 2048 in all
- left: bfloat16 [9, 384, 3072], P(None, 'lo', 'up'), may hold values from -6 to 6
- upper_edge: bfloat16 [9, 384, 3072], P(None, 'up', 'lo'), may hold values from -0.3125 to 0.3125
- lower_edge: bfloat16 [9, 384, 3072], P(None, 'up', 'lo'), may hold values from -0.109375 to 0.109375
- site_block: float32 [9, 9, 9, 9], replicated, may hold values from -1.5 to 1.5
Outputs:
- right: bfloat16 [9, 384, 3072], P(None, 'lo', 'up')
Inputs may be any that keep to these rules, and one draw needn't show every extreme that they name: `sector_sizes`: the 8 sector sizes sum to 2048, and the largest equals 384.
All inputs are finite; a program needn't handle non-finite values.
Results may differ from a plain program's by a relative error of at most 0.022.
Values may be sent and summed in bfloat16 or wider, within the bound.
No kernel may reach another device: no remote copies, remote signals or barrier semaphores. Data moves between devices by JAX's collectives and lax.ppermute only.
A program may use at most 128 MiB of HBM per device.

v0:
```python
import jax
import jax.numpy as jnp
from jax import lax
from jax.sharding import PartitionSpec as P

SEC = 8
DD = 9


def charge_list():
    return [member // 3 - member % 3 for member in range(DD)]


def allowed(sector_sizes, charges, row_ids, col_ids):
    slot_in = col_ids // SEC
    sector_in = col_ids % SEC
    labels = jnp.arange(SEC, dtype=jnp.int32)
    lookup_in = jnp.sum(
        jnp.where(sector_in[:, None] == labels[None, :], sector_sizes[None, :], 0), axis=1
    )
    live_in = slot_in < lookup_in
    sector_out = sector_in[None, :] + charges[:, None]
    lookup_out = jnp.sum(
        jnp.where(sector_out[:, :, None] == labels[None, None, :], sector_sizes[None, None, :], 0),
        axis=2,
    )
    live_out = row_ids[None, :, None] < lookup_out[:, None, :]
    return live_in[None, None, :] & live_out


def site_allowed(charges):
    charge_up = charges[:, None, None, None]
    charge_left = charges[None, :, None, None]
    charge_right = charges[None, None, :, None]
    charge_down = charges[None, None, None, :]
    return charge_up + charge_right == charge_left + charge_down


def move_along(values, amount, axis):
    if amount == 0:
        return values
    count = values.shape[axis]
    filler_shape = list(values.shape)
    filler_shape[axis] = abs(amount)
    filler = jnp.zeros(tuple(filler_shape), values.dtype)
    if amount > 0:
        kept = lax.slice_in_dim(values, 0, count - amount, 1, axis)
        return jnp.concatenate([filler, kept], axis=axis)
    kept = lax.slice_in_dim(values, -amount, count, 1, axis)
    return jnp.concatenate([kept, filler], axis=axis)


def widen_sectors(values, amount, axis):
    padding = [(0, 0)] * values.ndim
    padding[axis] = (2 + amount, 2 - amount)
    return jnp.pad(values, padding)


def sector_major(masked):
    depth, rows, width = masked.shape
    return masked.reshape(depth, rows, width // SEC, SEC).transpose(0, 1, 3, 2)


def contract_lower(lower_four, mixture, shifts):
    lower_wide = jnp.stack(
        [widen_sectors(lower_four[member], shifts[member], 1) for member in range(DD)]
    )
    mixed_wide = jnp.stack(
        [widen_sectors(mixture[member], shifts[member], 1) for member in range(DD)]
    )
    summed = jnp.einsum(
        "lyvj,plvjx->pvyx", lower_wide, mixed_wide, preferred_element_type=jnp.float32
    )
    pieces = [
        lax.slice_in_dim(summed[member], 2 + shifts[member], 2 + shifts[member] + SEC, 1, 0)
        for member in range(DD)
    ]
    return jnp.stack(pieces)


def fetch_lower(lower_masked):
    return lax.all_gather(sector_major(lower_masked), "up", axis=1, tiled=True)


def local(sector_sizes, left, upper_edge, lower_edge, site_block):
    shifts = charge_list()
    charges = jnp.array(shifts, dtype=jnp.int32)
    naught = jnp.zeros((), jnp.bfloat16)
    vec_rows = left.shape[1]
    vec_cols = left.shape[2]
    row_ids = lax.axis_index("lo") * vec_rows + jnp.arange(vec_rows, dtype=jnp.int32)
    col_ids = lax.axis_index("up") * vec_cols + jnp.arange(vec_cols, dtype=jnp.int32)
    vector = jnp.where(allowed(sector_sizes, charges, row_ids, col_ids), left, naught)
    edge_rows = upper_edge.shape[1]
    edge_cols = upper_edge.shape[2]
    edge_row_ids = lax.axis_index("up") * edge_rows + jnp.arange(edge_rows, dtype=jnp.int32)
    edge_col_ids = lax.axis_index("lo") * edge_cols + jnp.arange(edge_cols, dtype=jnp.int32)
    edge_mask = allowed(sector_sizes, charges, edge_row_ids, edge_col_ids)
    upper_masked = jnp.where(edge_mask, upper_edge, naught)
    lower_masked = jnp.where(edge_mask, lower_edge, naught)
    site_tensor = jnp.where(site_allowed(charges), site_block, jnp.float32(0.0))
    upper_whole = lax.all_gather(sector_major(upper_masked), "lo", axis=3, tiled=True)
    vector_whole = lax.all_gather(sector_major(vector), "up", axis=3, tiled=True)
    product = jnp.einsum(
        "kxqi,sjqi->ksqjx", upper_whole, vector_whole, preferred_element_type=jnp.float32
    )
    product = jnp.stack([move_along(product[member], shifts[member], 1) for member in range(DD)])
    mixture = jnp.einsum(
        "kspl,ksqjx->plqjx", site_tensor, product, precision=lax.Precision.HIGHEST
    ).astype(jnp.bfloat16)
    lower_whole = fetch_lower(lower_masked)
    partial_value = contract_lower(lower_whole, mixture, shifts)
    result = lax.psum_scatter(
        partial_value.astype(jnp.bfloat16), "lo", scatter_dimension=2, tiled=True
    ).astype(jnp.float32)
    result = result.transpose(0, 2, 3, 1)
    return result.reshape(DD, result.shape[1], edge_rows * SEC).astype(jnp.bfloat16)


def solution(mesh):
    return jax.shard_map(
        local,
        mesh=mesh,
        in_specs=(P(), P(None, "lo", "up"), P(None, "up", "lo"), P(None, "up", "lo"), P()),
        out_specs=P(None, "lo", "up"),
        check_vma=False,
    )
```

profile of v0, /device:TPU:1, one launch (start us, length us, event | category | flops | bytes accessed | tf_op | source)
XLA Modules:
  0.0 373.2 jit_solution(14227819757473286767)
XLA Ops:
  8.8 1.0 copy.73
  13.1 1.0 fusion.28
  14.6 0.9 copy.86
  17.0 1.4 copy.75
  18.3 56.4 %all_gather.10 = bf16[9,12,8,384]{1,2,0,3:T(8,128)(2,1)} all-gather(bf16[9,12,8,24]{1,2,0,3:T(8,128)(2,1)S(1)} %copy.75), channel_id=1, replica_groups=mesh['up'=32,'lo'=16] {'lo'}, dimensions={3}, use_global_device_ids=true | all-gather | bytes 705024 | tf_op jit(solution)/shard_map/all_gather | solution.py:102
  74.8 38.2 %all-gather.3.cloned.1.call-done = bf16[9,24,8,384]{1,2,0,3:T(8,128)(2,1)} async-done(((bf16[9,24,8,12]{1,2,0,3:T(8,128)(2,1)}), bf16[9,24,8,384]{1,2,0,3:T(8,128)(2,1)}) %all-gather.3.cloned.1.call-update) | async-done | bytes 1327120 | tf_op jit(solution)/shard_map/all_gather | solution.py:103
  113.1 11.3 %fusion.10 = f32[9,9,8,24,12]{3,4,0,1,2:T(8,128)} fusion(bf16[9,12,8,384,1]{1,2,0,3,4:T(8,128)(2,1)} %bitcast.145, bf16[9,24,8,384,1]{1,2,0,3,4:T(8,128)(2,1)} %bitcast.146), kind=kOutput, calls=%fused_computation.10 | convolution fusion | flops 143327232 | bytes 2737152 | tf_op jit(solution)/shard_map/kxqi,sjqi->ksqjx/dot_general | solution.py:104
  124.3 2.6 slice_bitcast_fusion
  127.3 1.1 slice_dynamic-update-slice_fusion.1
  128.6 1.1 slice_dynamic-update-slice_fusion
  129.8 8.5 %bitcast_convert_fusion = bf16[9,9,8,24,12]{3,1,4,2,0:T(8,128)(2,1)S(1)} fusion(f32[9,9,8,24,12]{3,4,0,1,2:T(8,128)S(1)} %slice_dynamic-update-slice_fusion, f32[9,9,9,9,1,1]{3,2,1,0,5,4:T(8,128)S(1)} %select_bitcast_fusion), kind=kOutput, calls=%fused_computation | convolution fusion | flops 181585152 | bytes 1145988 | tf_op jit(solution)/shard_map/kspl,ksqjx->plqjx/dot_general | solution.py:108
  138.2 1.7 slice_bitcast_fusion.6
  140.9 70.2 %all-gather.5.cloned.1.call-done = bf16[9,384,8,24]{3,2,0,1:T(8,128)(2,1)} async-done(((bf16[9,12,8,24]{3,2,0,1:T(8,128)(2,1)}), bf16[9,384,8,24]{3,2,0,1:T(8,128)(2,1)}) %all-gather.5.cloned.1.call-update) | async-done | bytes 1327120 | tf_op jit(solution)/shard_map/all_gather | solution.py:82
  211.1 5.1 %fusion.32 = (bf16[1,384,8,24]{3,2,0,1:T(8,128)(2,1)S(1)}, bf16[1,384,8,24]{3,2,0,1:T(8,128)(2,1)S(1)}, bf16[1,384,8,24]{3,2,0,1:T(8,128)(2,1)S(1)}, bf16[1,384,...) fusion(bf16[9,384,8,24]{3,2,0,1:T(8,128)(2,1)} %all-gather.5.cl, ...), kind=kLoop, calls=%fused_computation.102 | loop fusion | bytes 2654208 | tf_op jit(solution)/shard_map/slice | solution.py:66
  216.1 2.2 copy.119
  218.3 1.6 bitcast_dynamic-update-slice_fusion.23
  220.0 2.2 copy.120
  222.2 2.2 copy.121
  224.3 2.2 copy.122
  226.5 2.2 copy.123
  228.7 1.1 copy.124
  229.8 1.1 copy.125
  232.0 2.1 bitcast_dynamic-update-slice_fusion.7
  234.1 2.0 bitcast_dynamic-update-slice_fusion.6
  236.0 2.0 bitcast_dynamic-update-slice_fusion.5
  238.0 1.9 bitcast_dynamic-update-slice_fusion.4
  239.9 0.9 bitcast_dynamic-update-slice_fusion.3
  242.8 0.9 bitcast_dynamic-update-slice_fusion
  244.1 4.0 %fusion.20 = bf16[9,12,384,12]{2,3,0,1:T(8,128)(2,1)S(1)} fusion(bf16[9,384,12,24]{1,3,0,2:T(8,128)(2,1)S(1)} %bitcast_dynamic-update-slice_fusion.15, bf16[9,9,12,24,12]{3,1,4,2,0:T(8,128)(2,1)} %bitcast_dynamic-update-slice_fusion), kind=kOutput, calls=%fused_computation.12 | convolution fusion | flops 215488512 | bytes 3545856 | tf_op jit(solution)/shard_map/lyvj,plvjx->pvyx/dot_general | solution.py:71
  249.2 1.3 dynamic-slice
  251.2 113.5 %all-reduce.27.cloned.1.call-done = bf16[9,8,384,12]{2,3,0,1:T(8,128)(2,1)} async-done(((bf16[9,8,384,12]{2,3,0,1:T(8,128)(2,1)}), bf16[9,8,384,12]{2,3,0,1:T(8,128)(2,1)}) %all-reduce.27.cloned.1.call-update) | async-done | bytes 663568
  364.6 1.2 dynamic-slice_bitcast_fusion
  (84 shorter events, 13.9 us)
Async XLA Ops:
  6.5 106.5 %all-gather.3.cloned.1.call-start = ((), (), s32[]{:S(2)}) async-start(), calls=%async_computation | async-start | bytes 7299072 | tf_op jit(solution)/shard_map/all_gather | solution.py:103
  10.8 200.3 %all-gather.5.cloned.1.call-start = ((), (), s32[]{:S(2)}) async-start(), calls=%async_computation.1 | async-start | bytes 7299072 | tf_op jit(solution)/shard_map/all_gather | solution.py:82
  14.6 60.1 %copy-start.4 = (f32[9,9,9,9]{3,2,1,0:T(8,128)S(1)}, f32[9,9,9,9]{3,2,1,0:T(8,128)}, u32[]{:S(2)}) copy-start(f32[9,9,9,9]{3,2,1,0:T(8,128)} %param.10) | copy-start | bytes 78736
  15.6 349.0 %all-reduce.27.cloned.1.call-start = ((), (), s32[]{:S(2)}) async-start(), calls=%async_computation.2 | async-start | bytes 1769472
  229.8 11.1 %copy-start.1 = (bf16[9,8,24,12]{2,0,3,1:T(8,128)(2,1)S(1)}, bf16[9,8,24,12]{2,0,3,1:T(8,128)(2,1)}, u32[]{:S(2)}) copy-start(bf16[9,8,24,12]{2,0,3,1:T(8,128)(2,1)} %get-tuple-element.23) | copy-start | bytes 124420
  229.8 12.0 %copy-start = (bf16[9,8,24,12]{2,0,3,1:T(8,128)(2,1)S(1)}, bf16[9,8,24,12]{2,0,3,1:T(8,128)(2,1)}, u32[]{:S(2)}) copy-start(bf16[9,8,24,12]{2,0,3,1:T(8,128)(2,1)} %get-tuple-element.22) | copy-start | bytes 124420
  230.9 9.0 %copy-start.2 = (bf16[9,8,24,12]{2,0,3,1:T(8,128)(2,1)S(1)}, bf16[9,8,24,12]{2,0,3,1:T(8,128)(2,1)}, u32[]{:S(2)}) copy-start(bf16[9,8,24,12]{2,0,3,1:T(8,128)(2,1)} %get-tuple-element.24) | copy-start | bytes 124420
  231.4 12.3 %copy-start.9 = (bf16[1,384,8,24]{1,3,2,0:T(8,128)(2,1)S(1)}, bf16[1,384,8,24]{1,3,2,0:T(8,128)(2,1)}, u32[]{:S(2)}) copy-start(bf16[1,384,8,24]{1,3,2,0:T(8,128)(2,1)} %copy.120) | copy-start | bytes 442372
  231.4 12.4 %copy-start.8 = (bf16[1,384,8,24]{1,3,2,0:T(8,128)(2,1)S(1)}, bf16[1,384,8,24]{1,3,2,0:T(8,128)(2,1)}, u32[]{:S(2)}) copy-start(bf16[1,384,8,24]{1,3,2,0:T(8,128)(2,1)} %copy.122) | copy-start | bytes 442372
  231.4 12.4 %copy-start.7 = (bf16[1,384,8,24]{1,3,2,0:T(8,128)(2,1)S(1)}, bf16[1,384,8,24]{1,3,2,0:T(8,128)(2,1)}, u32[]{:S(2)}) copy-start(bf16[1,384,8,24]{1,3,2,0:T(8,128)(2,1)} %copy.123) | copy-start | bytes 442372
  231.4 12.4 %copy-start.6 = (bf16[1,384,8,24]{1,3,2,0:T(8,128)(2,1)S(1)}, bf16[1,384,8,24]{1,3,2,0:T(8,128)(2,1)}, u32[]{:S(2)}) copy-start(bf16[1,384,8,24]{1,3,2,0:T(8,128)(2,1)} %copy.124) | copy-start | bytes 442372
  231.5 12.5 %copy-start.5 = (bf16[1,384,8,24]{1,3,2,0:T(8,128)(2,1)S(1)}, bf16[1,384,8,24]{1,3,2,0:T(8,128)(2,1)}, u32[]{:S(2)}) copy-start(bf16[1,384,8,24]{1,3,2,0:T(8,128)(2,1)} %copy.125) | copy-start | bytes 442372
  231.9 11.8 %copy-start.11 = (bf16[9,384,12,24]{1,3,0,2:T(8,128)(2,1)S(1)}, bf16[9,384,12,24]{1,3,0,2:T(8,128)(2,1)}, u32[]{:S(2)}) copy-start(bf16[9,384,12,24]{1,3,0,2:T(8,128)(2,1)} %bitcast_dynamic-update-slice_fusion.23) | copy-start | bytes 5971972
  232.0 11.8 %copy-start.10 = (bf16[1,384,8,24]{1,3,2,0:T(8,128)(2,1)S(1)}, bf16[1,384,8,24]{1,3,2,0:T(8,128)(2,1)}, u32[]{:S(2)}) copy-start(bf16[1,384,8,24]{1,3,2,0:T(8,128)(2,1)} %copy.121) | copy-start | bytes 442372
  248.3 0.9 copy-start.3
Sparse Core Ops, SparseCore 0:
  10.9 102.1 all-gather.2
  116.2 94.7 all-gather.4
  249.4 115.2 all-reduce.26
where the time goes:
time: 374 us; the launch traced here: 373 us
  waiting for transfers between devices  222 us (59%)
  blocking collectives  56.4 us (15%)
  local copies, waits for them, and re-layouts  50.2 us (13%)
  matrix products  23.7 us (6%)
  between operations  14.2 us (4%)
  other arithmetic  6.66 us (2%)
    unnamed x4, waiting for transfers between devices  114 us
    all_gather x1, waiting for transfers between devices, fetch_lower(): return lax.all_gather(sector_major(lower_masked), 'up', axis=1, tiled=True)  70.2 us
    all_gather x1, blocking collectives, local(): lax.all_gather(sector_major(upper_masked), 'lo', axis=3, tiled=True)  56.4 us
    all_gather x1, waiting for transfers between devices, local(): lax.all_gather(sector_major(vector), 'up', axis=3, tiled=True)  38.2 us
    unnamed x66, local copies, waits for them, and re-layouts  32.4 us
    dot_general x1, matrix products, local(): jnp.einsum('kxqi,sjqi->ksqjx', upper_whole, vector_whole, preferred_eleme...  11.3 us
    dot_general x1, matrix products, local(): jnp.einsum('kspl,ksqjx->plqjx', site_tensor, product, precision=lax.Preci...  8.47 us
  transfers between devices with their start and end apart: 3, of which 3 were waited for; matrix products, arithmetic and copies ran while one was open for 10% of the time, Pallas kernels for 0%

commit v1 on v0

v1 whole, which is shorter than its diff:
```python
import jax
import jax.numpy as jnp
from jax import lax
from jax.experimental import pallas as pl
from jax.experimental.pallas import tpu as pltpu
from jax.sharding import PartitionSpec as P

SEC = 8
DD = 9
NX = 4
NY = 8
N_UP = NX * NY
N_LO = 16
XB = 12
JB = 24
CAP = 384
CHARGE = [member // 3 - member % 3 for member in range(DD)]
ORDER = [0, 1, 2, 3, 5, 4, 6, 7, 8]


def places(charge):
    free = [(q, a) for q in range(SEC) for a in range(SEC) if not 0 <= q + charge[ORDER[a]] < SEC]
    found = [None] * SEC
    for q in range(SEC):
        own = [spot for spot in free if spot[0] == q]
        if own:
            found[q] = own[0]
            free.remove(own[0])
    for q in range(SEC):
        if found[q] is None:
            found[q] = free.pop(0)
    return found


IN_PLACES = places(CHARGE)
OUT_PLACES = places([-c for c in CHARGE])
BF = jnp.bfloat16
F32 = jnp.float32
VMEM = pl.BlockSpec(memory_space=pltpu.VMEM)
SMEM = pl.BlockSpec(memory_space=pltpu.SMEM)
PARAMS = pltpu.CompilerParams(vmem_limit_bytes=56 * 1024 * 1024)


def nt(a, b):
    return lax.dot_general(a, b, (((1,), (1,)), ((), ())), preferred_element_type=F32)


def nn(a, b):
    return lax.dot_general(a, b, (((1,), (0,)), ((), ())), preferred_element_type=F32)


def tn(a, b):
    return lax.dot_general(a, b, (((0,), (0,)), ((), ())), preferred_element_type=F32)


def iota(shape, axis):
    return lax.broadcasted_iota(jnp.int32, shape, axis)


def one_hot(flag):
    return jnp.where(flag, 1.0, 0.0).astype(BF)


def sizes_by_sector(sizes_ref, sector, charge):
    found = jnp.zeros(sector.shape, jnp.int32)
    for q in range(SEC):
        if 0 <= q + charge < SEC:
            found = jnp.where(sector == q, sizes_ref[q + charge], found)
    return found


def prepare_kernel(sizes, place, left, upper, lower, lb_out, u_out, left_s, up_s, wide_s, pack):
    up, lo = place[0], place[1]
    lane = iota((1, XB * SEC), 1)
    live = up * XB + lane // SEC < sizes_by_sector(sizes, lane % SEC, 0)
    row = lo * JB + iota((JB, 1), 0)
    limit = {c: sizes_by_sector(sizes, lane % SEC, c) for c in sorted(set(CHARGE))}
    for a, s in enumerate(ORDER):
        keep = live & (row < limit[CHARGE[s]])
        left_s[a * JB:(a + 1) * JB, :] = jnp.where(keep, left[s].astype(F32), 0.0)
    a, b = iota((96, 96), 0), iota((96, 96), 1)
    order = one_hot(b == (a % XB) * SEC + a // XB)
    grid = nt(order, left_s[...].astype(BF))
    pack[0] = grid[:, 0:192]
    for q, (host, at) in enumerate(IN_PLACES):
        pack[0, host * XB:(host + 1) * XB, at * JB:(at + 1) * JB] = grid[q * XB:(q + 1) * XB, 192:216]
    lane = iota((1, JB * SEC), 1)
    live = lo * JB + lane // SEC < sizes_by_sector(sizes, lane % SEC, 0)
    row = up * XB + iota((XB, 1), 0)
    limit = {c: sizes_by_sector(sizes, lane % SEC, c) for c in sorted(set(CHARGE))}
    blank = jnp.zeros((4, JB * SEC), F32)
    for k in range(DD):
        keep = live & (row < limit[CHARGE[k]])
        up_s[0, k * 16:k * 16 + XB, :] = jnp.where(keep, upper[k].astype(F32), 0.0)
        up_s[0, k * 16 + XB:(k + 1) * 16, :] = blank
        up_s[1, k * 16:k * 16 + XB, :] = jnp.where(keep, lower[k].astype(F32), 0.0)
        up_s[1, k * 16 + XB:(k + 1) * 16, :] = blank
    a, b = iota((128, 144), 0), iota((128, 144), 1)
    dense = nn(one_hot((b == (a // XB) * 16 + a % XB) & (a < 108)), up_s[0].astype(BF)).astype(BF)
    a, b = iota((192, 192), 0), iota((192, 192), 1)
    edge = nt(one_hot(b == (a % JB) * SEC + a // JB), dense).astype(BF)
    a, b = iota((96, 144), 0), iota((96, 144), 1)
    lower_16 = up_s[1].astype(BF)
    sector = iota((96, 192), 0) // XB
    column = iota((96, 192), 1) % SEC
    for n, l in enumerate(ORDER):
        copies = nn(one_hot(b == l * 16 + a % XB), lower_16)
        wide_s[:, n * 256:n * 256 + 192] = jnp.where(
            column == sector - CHARGE[l], copies, 0.0
        ).astype(BF)
        wide_s[:, n * 256 + 192:(n + 1) * 256] = jnp.zeros((96, 64), BF)
    a, b = iota((DD * 256, 256), 0), iota((DD * 256, 256), 1)
    fold = one_hot(b == (a // 256) * JB + (a % 256) // SEC)
    grid = nn(wide_s[...], fold)
    pack[1] = grid[:, 0:192]
    for v, (host, at) in enumerate(OUT_PLACES):
        pack[1, host * XB:(host + 1) * XB, at * JB:(at + 1) * JB] = grid[v * XB:(v + 1) * XB, 192:216]
    ours = pack[0].astype(BF)
    theirs = pack[1].astype(BF)
    for n in range(NY):
        lb_out[n, 0:96, :] = ours[:, 0:128]
        lb_out[n, 96:192, :] = theirs[:, 0:128]
        lb_out[n, 192:288, 0:64] = ours[:, 128:192]
        lb_out[n, 192:288, 64:128] = theirs[:, 128:192]
    u_out[...] = edge


def prepare(sizes, place, left, upper, lower):
    return pl.pallas_call(
        prepare_kernel,
        out_shape=(
            jax.ShapeDtypeStruct((NY, 288, 128), BF),
            jax.ShapeDtypeStruct((192, 128), BF),
        ),
        in_specs=[SMEM, SMEM, VMEM, VMEM, VMEM],
        out_specs=(VMEM, VMEM),
        scratch_shapes=[
            pltpu.VMEM((216, 96), F32),
            pltpu.VMEM((2, 144, 192), F32),
            pltpu.VMEM((96, DD * 256), BF),
            pltpu.VMEM((2, 96, 192), F32),
        ],
        compiler_params=PARAMS,
        name="prepare",
    )(sizes, place, left, upper, lower)


def lanes_of(at, side):
    start = at * JB
    return side * 128 + start if start + JB <= 128 else 256 + side * 64 + start - 128


def main_kernel(site, lb, u, out, left_q, lower_v, image, at, mixed, spread):
    a, b = iota((384, 384), 0), iota((384, 384), 1)
    regroup = one_hot(b == ((a % 48) // XB) * 96 + (a // 48) * XB + a % XB)
    lane = iota((1, 256), 1) // JB
    zero = jnp.zeros((), BF)
    left_q[...] = jnp.zeros(left_q.shape, BF)
    lower_v[...] = jnp.zeros(lower_v.shape, BF)
    for g in range(NY):
        block = jnp.concatenate(
            [lb[:, g, 96 * n:96 * (n + 1), :].reshape(384, 128) for n in range(3)], axis=1
        )
        part = nn(regroup, block).astype(BF)
        rows = slice(g * 48, (g + 1) * 48)
        for q in range(SEC):
            near = part[q * 48:(q + 1) * 48, 0:128]
            far = part[q * 48:(q + 1) * 48, 256:320]
            empty = [n for n in range(SEC) if not 0 <= q + CHARGE[ORDER[n]] < SEC]
            for n in empty:
                near = jnp.where(lane[:, 0:128] == n, zero, near)
                far = jnp.where(lane[:, 128:192] == n, zero, far)
            left_q[q, rows, 0:128] = near
            left_q[q, rows, 128:192] = far
            host, spot = IN_PLACES[q]
            start = lanes_of(spot, 0)
            left_q[q, rows, 192:216] = part[host * 48:(host + 1) * 48, start:start + JB]
        for v in range(SEC):
            near = part[v * 48:(v + 1) * 48, 128:256]
            far = part[v * 48:(v + 1) * 48, 320:384]
            empty = [n for n in range(SEC) if not 0 <= v - CHARGE[ORDER[n]] < SEC]
            for n in empty:
                near = jnp.where(lane[:, 0:128] == n, zero, near)
                far = jnp.where(lane[:, 128:192] == n, zero, far)
            lower_v[rows, v * 256:v * 256 + 128] = near
            lower_v[rows, v * 256 + 128:v * 256 + 192] = far
            host, spot = OUT_PLACES[v]
            start = lanes_of(spot, 1)
            lower_v[rows, v * 256 + 192:v * 256 + 216] = part[host * 48:(host + 1) * 48, start:start + JB]
    for q in range(SEC):
        columns = u[:, q * JB:(q + 1) * JB, :].reshape(CAP, 128)
        image[q * 128:(q + 1) * 128, :] = tn(columns, left_q[q]).astype(BF)
    a, b = iota((96, 1024), 0), iota((96, 1024), 1)
    p, x = a // XB, a % XB
    for k in range(DD):
        q = p - CHARGE[k]
        pick = one_hot((b == q * 128 + k * XB + x) & (q >= 0) & (q < SEC))
        at[:, k * 256:(k + 1) * 256] = nn(pick, image[...]).astype(BF)
    a, b = iota((81, DD * 256), 0), iota((81, DD * 256), 1)
    pos = (b % 256) // JB
    s = jnp.where(pos == 4, ORDER[4], jnp.where(pos == 5, ORDER[5], pos))
    widen = one_hot((s + (b // 256) * DD == a) & (pos < DD))
    weights = nn(site[...].astype(BF), widen)
    a, b = iota((JB, DD * 256), 0), iota((JB, DD * 256), 1)
    same = ((b % 256) % JB == a) & (b % 256 < 216)
    mixed[216:256, :] = jnp.zeros((40, SEC * 96), BF)
    last = None
    for n, r in enumerate(ORDER):
        rows = [
            jnp.where(same, weights[r * DD + l:r * DD + l + 1, :], 0.0).astype(BF) for l in ORDER
        ]
        last = nt(jnp.concatenate(rows, axis=0), at[...]).astype(BF)
        if n < SEC:
            mixed[0:216, n * 96:(n + 1) * 96] = last
    for p, (host, spot) in enumerate(IN_PLACES):
        start = spot * 96 + host * XB
        mixed[0:216, start:start + XB] = last[:, p * XB:(p + 1) * XB]
    lane = iota((1, SEC * 96), 1)
    sector = (lane % 96) // XB
    for n in range(SEC):
        sector = jnp.where(lane // 96 == n, sector + CHARGE[ORDER[n]], sector)
    for p, (host, spot) in enumerate(IN_PLACES):
        sector = jnp.where(lane // XB == spot * SEC + host, p, sector)
    for v in range(SEC):
        spread[v * 256:(v + 1) * 256, :] = jnp.where(sector == v, mixed[...], zero)
    for n in range(3):
        cut = slice(n * 256, (n + 1) * 256)
        out[:, cut] = nn(lower_v[...], spread[:, cut]).astype(BF)


def main(site, lb, u):
    return pl.pallas_call(
        main_kernel,
        out_shape=jax.ShapeDtypeStruct((CAP, SEC * 96), BF),
        in_specs=[VMEM] * 3,
        out_specs=VMEM,
        scratch_shapes=[
            pltpu.VMEM((SEC, CAP, 256), BF),
            pltpu.VMEM((CAP, SEC * 256), BF),
            pltpu.VMEM((SEC * 128, 256), BF),
            pltpu.VMEM((96, DD * 256), BF),
            pltpu.VMEM((256, SEC * 96), BF),
            pltpu.VMEM((SEC * 256, SEC * 96), BF),
        ],
        compiler_params=PARAMS,
        name="main",
    )(site, lb, u)


def finish_kernel(terms, out, stacked):
    total = terms[0].astype(F32)
    for z in range(1, N_LO):
        total = total + terms[z].astype(F32)
    for n in range(SEC):
        r = ORDER[n]
        stacked[r * JB:(r + 1) * JB, :] = total[:, n * 96:(n + 1) * 96]
    for p, (host, spot) in enumerate(IN_PLACES):
        start = spot * 96 + host * XB
        stacked[SEC * JB:DD * JB, p * XB:(p + 1) * XB] = total[:, start:start + XB]
    a, b = iota((96, 96), 0), iota((96, 96), 1)
    turned = nn(stacked[...].astype(BF), one_hot(b == (a % XB) * SEC + a // XB))
    p = iota((1, 96), 1) % SEC
    for r in range(DD):
        keep = (p + CHARGE[r] >= 0) & (p + CHARGE[r] < SEC)
        out[r] = jnp.where(keep, turned[r * JB:(r + 1) * JB, :], 0.0).astype(BF)


def finish(terms):
    return pl.pallas_call(
        finish_kernel,
        out_shape=jax.ShapeDtypeStruct((DD, JB, 96), BF),
        in_specs=[VMEM],
        out_specs=VMEM,
        scratch_shapes=[pltpu.VMEM((DD * JB, 96), F32)],
        compiler_params=PARAMS,
        name="finish",
    )(terms)


X_GROUPS = [[y * NX + x for x in range(NX)] for y in range(NY)]
Y_GROUPS = [[y * NX + x for y in range(NY)] for x in range(NX)]


def local(sector_sizes, left, upper_edge, lower_edge, site_block):
    charges = jnp.array(CHARGE, dtype=jnp.int32)
    place = jnp.stack([lax.axis_index("up"), lax.axis_index("lo")]).astype(jnp.int32)
    even = (
        charges[:, None, None, None] + charges[None, None, :, None]
        == charges[None, :, None, None] + charges[None, None, None, :]
    )
    site = jnp.where(even, site_block, jnp.float32(0.0))
    site = site.transpose(2, 3, 0, 1).reshape(81, 81)
    lb, u = prepare(sector_sizes, place, left, upper_edge, lower_edge)
    line = lax.all_to_all(lb, "up", 0, 0, axis_index_groups=Y_GROUPS)
    line, u, site = lax.optimization_barrier((line, u, site))
    whole = lax.all_to_all(
        jnp.broadcast_to(line, (NX,) + line.shape), "up", 0, 0, axis_index_groups=X_GROUPS
    )
    u = lax.all_gather(u, "lo", axis=0)
    terms = main(site, whole, u)
    terms = lax.all_to_all(terms.reshape(N_LO, JB, SEC * 96), "lo", 0, 0)
    return finish(terms)


def solution(mesh):
    return jax.shard_map(
        local,
        mesh=mesh,
        in_specs=(P(), P(None, "lo", "up"), P(None, "up", "lo"), P(None, "up", "lo"), P()),
        out_specs=P(None, "lo", "up"),
        check_vma=False,
    )
```

time: 374 us -> 111 us (0.30)
  waiting for transfers between devices: 222 us -> 14.7 us
  local copies, waits for them, and re-layouts: 50.2 us -> 4.09 us
  matrix products: 23.7 us -> 0 us
  Pallas kernels: 0 us -> 16.1 us
  starting transfers between devices: 0.09 us -> 14.7 us
  between operations: 14.2 us -> 0.02 us
  other arithmetic: 6.66 us -> 2.6 us
    unnamed x4 -> x0, waiting for transfers between devices: 114 us -> none
    all_gather x2 -> x0, waiting for transfers between devices: 108 us -> none  [the longest x1 70.2 us: fetch_lower(): return lax.all_gather(sector_major(lower_masked), 'up', axis=1, tiled=True)]
    all_to_all x0 -> x1, blocking collectives: none -> 31 us  [local(): terms = lax.all_to_all(terms.reshape(N_LO, JB, SEC * 96), 'lo', 0, 0)]
    unnamed x66 -> x4, local copies, waits for them, and re-layouts: 32.4 us -> 1.41 us
    all_gather x1, blocking collectives: 56.4 us -> 27.3 us  [local(): u = lax.all_gather(u, 'lo', axis=0)]
    dot_general x3 -> x0, matrix products: 23.7 us -> none  [the longest x1 11.3 us: local(): jnp.einsum('kxqi,sjqi->ksqjx', upper_whole, vector_whole, preferred_eleme...]
    pallas_call x0 -> x3, Pallas kernels: none -> 16.1 us  [the longest x1 11.1 us: main(): pl.pallas_call(main_kernel, out_shape=jax.ShapeDtypeStruct((CAP, SEC * 96...]
    all_to_all x0 -> x2, starting transfers between devices: none -> 14.7 us  [the longest x1 7.66 us: local(): line = lax.all_to_all(lb, 'up', 0, 0, axis_index_groups=Y_GROUPS)]
  transfers between devices with their start and end apart: 3 -> 2, of which waited for: 3 -> 2; matrix products, arithmetic and copies ran while one was open for 10% -> 3% of each run, Pallas kernels for 0% -> 0%
where the time goes in v1:
time: 111 us; the launch traced here: 110 us
  blocking collectives  58.3 us (53%)
  Pallas kernels  16.1 us (15%)
  starting transfers between devices  14.7 us (13%)
  waiting for transfers between devices  14.7 us (13%)
  local copies, waits for them, and re-layouts  4.09 us (4%)
  other arithmetic  2.6 us (2%)
    all_to_all x1, blocking collectives, local(): terms = lax.all_to_all(terms.reshape(N_LO, JB, SEC * 96), 'lo', 0, 0)  31 us
    all_gather x1, blocking collectives, local(): u = lax.all_gather(u, 'lo', axis=0)  27.3 us
    all_to_all x1, waiting for transfers between devices, local(): line = lax.all_to_all(lb, 'up', 0, 0, axis_index_groups=Y_GROUPS)  13.5 us
    pallas_call x1, Pallas kernels, main(): pl.pallas_call(main_kernel, out_shape=jax.ShapeDtypeStruct((CAP, SEC * 96...  11.1 us
    all_to_all x1, starting transfers between devices, local(): line = lax.all_to_all(lb, 'up', 0, 0, axis_index_groups=Y_GROUPS)  7.66 us
    all_to_all x1, starting transfers between devices, local(): lax.all_to_all(jnp.broadcast_to(line, (NX,) + line.shape), 'up', 0, 0, ax...  7.03 us
    pallas_call x1, Pallas kernels, prepare(): pl.pallas_call(prepare_kernel, out_shape=(jax.ShapeDtypeStruct((NY, 288,...  3.01 us
  transfers between devices with their start and end apart: 2, of which 2 were waited for; matrix products, arithmetic and copies ran while one was open for 3% of the time, Pallas kernels for 0%

profile of v1, /device:TPU:1, one launch (start us, length us, event | category | flops | bytes accessed | tf_op | source)
XLA Modules:
  0.0 110.5 jit_solution(12357758458335659932)
XLA Ops:
  0.0 0.6 pad_add_fusion.place
  0.6 3.0 %prepare.1 = (bf16[8,288,128]{2,1,0:T(8,128)(2,1)}, bf16[192,128]{1,0:T(8,128)(2,1)}) custom-call(s32[8]{0:T(128)} %sizes.1, s32[2]{0:T(128)} %pad_add_fusion.place, bf16[9,24,96]{2,1,0:T(8,128)(2,1)} %left.1, bf16[9,12,192]{2,1,0:T(8,128)(2,1)} %upper.1, bf16[9,12,192]{2,1,0:T(8,128)(2,1)} %lower.1), custom_call_target="tpu_custom_call" | custom-call | tf_op jit(solution)/shard_map/prepare/pallas_call | solution.py:129
  3.6 7.7 %all-to-all-start = ((bf16[8,288,128]{2,1,0:T(8,128)(2,1)}), bf16[8,288,128]{2,1,0:T(8,128)(2,1)S(1)}, u32[]{:S(2)}, u32[]{:S(2)}) async-start(bf16[8,288,128]{2,1,0:T(8,128)(2,1)} %get-tuple-element.10), calls=%async_computation | async-start | bytes 1179648 | tf_op jit(solution)/shard_map/all_to_all | solution.py:294
  11.3 0.8 broadcast_add_fusion
  12.1 1.2 %select_bitcast_fusion = f32[9,9,9,9]{1,0,3,2:T(8,128)S(1)} fusion(f32[9,9,9,9]{3,2,1,0:T(8,128)} %param.10, s32[9,9]{1,0:T(8,128)S(1)} %broadcast_add_fusion), kind=kLoop, calls=%fused_computation | loop fusion | flops 13122 | bytes 52812 | tf_op jit(solution)/shard_map/transpose | solution.py:292
  13.3 0.2 reshape.71
  13.5 0.7 copy.8.site
  14.2 13.5 %all-to-all-done = bf16[8,288,128]{2,1,0:T(8,128)(2,1)S(1)} async-done(((bf16[8,288,128]{2,1,0:T(8,128)(2,1)}), bf16[8,288,128]{2,1,0:T(8,128)(2,1)S(1)}, u32[]{:S(2)}, u32[]{:S(2)}) %all-to-all-start) | async-done | bytes 589856 | tf_op jit(solution)/shard_map/all_to_all | solution.py:294
  27.7 1.8 %broadcast_in_dim.12 = bf16[4,8,288,128]{3,2,1,0:T(8,128)(2,1)} broadcast(bf16[8,288,128]{2,1,0:T(8,128)(2,1)S(1)} %all-to-all-done), dimensions={1,2,3} | broadcast | bytes 2949120 | tf_op jit(solution)/shard_map/broadcast_in_dim | solution.py:297
  29.5 0.0 copy-start.1
  29.5 7.0 %all-to-all-start.1 = ((bf16[4,8,288,128]{3,2,1,0:T(8,128)(2,1)}), bf16[4,8,288,128]{3,2,1,0:T(8,128)(2,1)S(1)}, u32[]{:S(2)}, u32[]{:S(2)}) async-start(bf16[4,8,288,128]{3,2,1,0:T(8,128)(2,1)} %broadcast_in_dim.12), calls=%async_computation.1 | async-start | bytes 4718592 | tf_op jit(solution)/shard_map/all_to_all | solution.py:296
  36.5 0.0 copy-done.1
  36.5 27.3 %all-gather = bf16[3072,128]{1,0:T(8,128)(2,1)} all-gather(bf16[192,128]{1,0:T(8,128)(2,1)S(1)} %copy-done.1), channel_id=2, replica_groups=mesh['up'=32,'lo'=16] {'lo'}, dimensions={0}, use_global_device_ids=true | all-gather | bytes 835584 | tf_op jit(solution)/shard_map/all_gather | solution.py:299
  63.8 1.1 %all-to-all-done.1.lb = bf16[4,8,288,128]{3,2,1,0:T(8,128)(2,1)S(1)} async-done(((bf16[4,8,288,128]{3,2,1,0:T(8,128)(2,1)}), bf16[4,8,288,128]{3,2,1,0:T(8,128)(2,1)S(1)}, u32[]{:S(2)}, u32[]{:S(2)}) %all-to-all-start.1) | async-done | bytes 2359328 | tf_op jit(solution)/shard_map/all_to_all | solution.py:296
  65.0 0.0 copy-start
  65.0 1.4 %copy-done = bf16[4,8,288,128]{3,2,1,0:T(8,128)(2,1)} copy-done((bf16[4,8,288,128]{3,2,1,0:T(8,128)(2,1)}, bf16[4,8,288,128]{3,2,1,0:T(8,128)(2,1)S(1)}, u32[]{:S(2)}) %copy-start) | copy-done | bytes 2359320
  66.4 11.1 %main.1 = bf16[384,768]{1,0:T(8,128)(2,1)} custom-call(f32[81,81]{1,0:T(8,128)} %copy.8.site, bf16[4,8,288,128]{3,2,1,0:T(8,128)(2,1)} %copy-done, bf16[16,192,128]{2,1,0:T(8,128)(2,1)} %bitcast.8), custom_call_target="tpu_custom_call" | custom-call | tf_op jit(solution)/shard_map/main/pallas_call | solution.py:232
  77.4 31.0 %all_to_all.15.terms = bf16[16,24,768]{2,1,0:T(8,128)(2,1)} all-to-all(bf16[16,24,768]{2,1,0:T(8,128)(2,1)} %bitcast.9), channel_id=1, replica_groups=mesh['up'=32,'lo'=16] {'lo'}, dimensions={0} | all-to-all | bytes 1179648 | tf_op jit(solution)/shard_map/all_to_all | solution.py:301
  108.5 2.0 %finish.1 = bf16[9,24,96]{2,1,0:T(8,128)(2,1)} custom-call(bf16[16,24,768]{2,1,0:T(8,128)(2,1)} %all_to_all.15.terms), custom_call_target="tpu_custom_call" | custom-call | tf_op jit(solution)/shard_map/finish/pallas_call | solution.py:269
Async XLA Ops:
  3.6 24.1 %all-to-all-start = ((bf16[8,288,128]{2,1,0:T(8,128)(2,1)}), bf16[8,288,128]{2,1,0:T(8,128)(2,1)S(1)}, u32[]{:S(2)}, u32[]{:S(2)}) async-start(bf16[8,288,128]{2,1,0:T(8,128)(2,1)} %get-tuple-element.10), calls=%async_computation | async-start | bytes 1179648 | tf_op jit(solution)/shard_map/all_to_all | solution.py:294
  29.5 7.0 %copy-start.1 = (bf16[192,128]{1,0:T(8,128)(2,1)S(1)}, bf16[192,128]{1,0:T(8,128)(2,1)}, u32[]{:S(2)}) copy-start(bf16[192,128]{1,0:T(8,128)(2,1)} %get-tuple-element.14) | copy-start | bytes 147460
  29.5 35.5 %all-to-all-start.1 = ((bf16[4,8,288,128]{3,2,1,0:T(8,128)(2,1)}), bf16[4,8,288,128]{3,2,1,0:T(8,128)(2,1)S(1)}, u32[]{:S(2)}, u32[]{:S(2)}) async-start(bf16[4,8,288,128]{3,2,1,0:T(8,128)(2,1)} %broadcast_in_dim.12), calls=%async_computation.1 | async-start | bytes 4718592 | tf_op jit(solution)/shard_map/all_to_all | solution.py:296
  65.0 1.4 %copy-start = (bf16[4,8,288,128]{3,2,1,0:T(8,128)(2,1)}, bf16[4,8,288,128]{3,2,1,0:T(8,128)(2,1)S(1)}, u32[]{:S(2)}) copy-start(bf16[4,8,288,128]{3,2,1,0:T(8,128)(2,1)S(1)} %all-to-all-done.1.lb) | copy-start | bytes 7077892

commit v2 on v1

--- a/solution.py
+++ b/solution.py
@@ -38,7 +38,8 @@
 F32 = jnp.float32
 VMEM = pl.BlockSpec(memory_space=pltpu.VMEM)
 SMEM = pl.BlockSpec(memory_space=pltpu.SMEM)
-PARAMS = pltpu.CompilerParams(vmem_limit_bytes=56 * 1024 * 1024)
+PARAMS = pltpu.CompilerParams(vmem_limit_bytes=16 * 1024 * 1024)
+WIDE = pltpu.CompilerParams(vmem_limit_bytes=56 * 1024 * 1024)
 
 
 def nt(a, b):
@@ -69,8 +70,8 @@
     return found
 
 
-def prepare_kernel(sizes, place, left, upper, lower, lb_out, u_out, left_s, up_s, wide_s, pack):
-    up, lo = place[0], place[1]
+def prepare_kernel(sizes, left, upper, lower, lb_out, u_out, left_s, up_s, wide_s, pack):
+    up, lo = lax.axis_index("up"), lax.axis_index("lo")
     lane = iota((1, XB * SEC), 1)
     live = up * XB + lane // SEC < sizes_by_sector(sizes, lane % SEC, 0)
     row = lo * JB + iota((JB, 1), 0)
@@ -125,14 +126,14 @@
     u_out[...] = edge
 
 
-def prepare(sizes, place, left, upper, lower):
+def prepare(sizes, left, upper, lower):
     return pl.pallas_call(
         prepare_kernel,
         out_shape=(
             jax.ShapeDtypeStruct((NY, 288, 128), BF),
             jax.ShapeDtypeStruct((192, 128), BF),
         ),
-        in_specs=[SMEM, SMEM, VMEM, VMEM, VMEM],
+        in_specs=[SMEM, VMEM, VMEM, VMEM],
         out_specs=(VMEM, VMEM),
         scratch_shapes=[
             pltpu.VMEM((216, 96), F32),
@@ -140,75 +141,65 @@
             pltpu.VMEM((96, DD * 256), BF),
             pltpu.VMEM((2, 96, 192), F32),
         ],
-        compiler_params=PARAMS,
+        compiler_params=WIDE,
         name="prepare",
-    )(sizes, place, left, upper, lower)
-
-
-def lanes_of(at, side):
-    start = at * JB
-    return side * 128 + start if start + JB <= 128 else 256 + side * 64 + start - 128
-
-
-def main_kernel(site, lb, u, out, left_q, lower_v, image, at, mixed, spread):
+    )(sizes, left, upper, lower)
+
+
+def regrouping(turn):
     a, b = iota((384, 384), 0), iota((384, 384), 1)
-    regroup = one_hot(b == ((a % 48) // XB) * 96 + (a // 48) * XB + a % XB)
-    lane = iota((1, 256), 1) // JB
-    zero = jnp.zeros((), BF)
+    x = ((a % 48) // XB + turn) % NX
+    return one_hot(b == x * 96 + (a // 48) * XB + a % XB)
+
+
+def spread_out(part, charge, hosts, sector):
+    lane = iota((1, 192), 1) // JB
+    rows = part[sector * 48:(sector + 1) * 48]
+    for n in range(SEC):
+        if not 0 <= sector + charge[ORDER[n]] < SEC:
+            rows = jnp.where(lane == n, jnp.zeros((), BF), rows)
+    host, spot = hosts[sector]
+    return rows, part[host * 48:(host + 1) * 48, spot * JB:(spot + 1) * JB]
+
+
+def main_kernel(site, lb, u, ours, theirs, left_q, lower_v, moved, at, mixed, spread, wide):
+    regroup_left = regrouping(0)
+    regroup_lower = regrouping(2 * lax.rem(lax.axis_index("lo"), 2))
     left_q[...] = jnp.zeros(left_q.shape, BF)
     lower_v[...] = jnp.zeros(lower_v.shape, BF)
+    moved[...] = jnp.zeros(moved.shape, F32)
     for g in range(NY):
-        block = jnp.concatenate(
-            [lb[:, g, 96 * n:96 * (n + 1), :].reshape(384, 128) for n in range(3)], axis=1
-        )
-        part = nn(regroup, block).astype(BF)
+        near, other, far = [lb[:, g, 96 * n:96 * (n + 1), :].reshape(384, 128) for n in range(3)]
         rows = slice(g * 48, (g + 1) * 48)
+        part = nn(regroup_left, jnp.concatenate([near, far[:, 0:64]], axis=1)).astype(BF)
         for q in range(SEC):
-            near = part[q * 48:(q + 1) * 48, 0:128]
-            far = part[q * 48:(q + 1) * 48, 256:320]
-            empty = [n for n in range(SEC) if not 0 <= q + CHARGE[ORDER[n]] < SEC]
-            for n in empty:
-                near = jnp.where(lane[:, 0:128] == n, zero, near)
-                far = jnp.where(lane[:, 128:192] == n, zero, far)
-            left_q[q, rows, 0:128] = near
-            left_q[q, rows, 128:192] = far
-            host, spot = IN_PLACES[q]
-            start = lanes_of(spot, 0)
-            left_q[q, rows, 192:216] = part[host * 48:(host + 1) * 48, start:start + JB]
+            own, last = spread_out(part, CHARGE, IN_PLACES, q)
+            left_q[q, rows, 0:192] = own
+            left_q[q, rows, 192:216] = last
+        part = nn(regroup_lower, jnp.concatenate([other, far[:, 64:128]], axis=1)).astype(BF)
         for v in range(SEC):
-            near = part[v * 48:(v + 1) * 48, 128:256]
-            far = part[v * 48:(v + 1) * 48, 320:384]
-            empty = [n for n in range(SEC) if not 0 <= v - CHARGE[ORDER[n]] < SEC]
-            for n in empty:
-                near = jnp.where(lane[:, 0:128] == n, zero, near)
-                far = jnp.where(lane[:, 128:192] == n, zero, far)
-            lower_v[rows, v * 256:v * 256 + 128] = near
-            lower_v[rows, v * 256 + 128:v * 256 + 192] = far
-            host, spot = OUT_PLACES[v]
-            start = lanes_of(spot, 1)
-            lower_v[rows, v * 256 + 192:v * 256 + 216] = part[host * 48:(host + 1) * 48, start:start + JB]
+            own, last = spread_out(part, [-c for c in CHARGE], OUT_PLACES, v)
+            lower_v[rows, v * 256:v * 256 + 192] = own
+            lower_v[rows, v * 256 + 192:v * 256 + 216] = last
     for q in range(SEC):
         columns = u[:, q * JB:(q + 1) * JB, :].reshape(CAP, 128)
-        image[q * 128:(q + 1) * 128, :] = tn(columns, left_q[q]).astype(BF)
-    a, b = iota((96, 1024), 0), iota((96, 1024), 1)
-    p, x = a // XB, a % XB
-    for k in range(DD):
-        q = p - CHARGE[k]
-        pick = one_hot((b == q * 128 + k * XB + x) & (q >= 0) & (q < SEC))
-        at[:, k * 256:(k + 1) * 256] = nn(pick, image[...]).astype(BF)
+        image = tn(columns, left_q[q])
+        for k in range(DD):
+            p = q + CHARGE[k]
+            if 0 <= p < SEC:
+                moved[p * XB:(p + 1) * XB, k * 256:(k + 1) * 256] = image[k * XB:(k + 1) * XB]
+    at[...] = moved[...].astype(BF)
     a, b = iota((81, DD * 256), 0), iota((81, DD * 256), 1)
     pos = (b % 256) // JB
     s = jnp.where(pos == 4, ORDER[4], jnp.where(pos == 5, ORDER[5], pos))
     widen = one_hot((s + (b // 256) * DD == a) & (pos < DD))
-    weights = nn(site[...].astype(BF), widen)
+    wide[...] = nn(site[...].astype(BF), widen)
     a, b = iota((JB, DD * 256), 0), iota((JB, DD * 256), 1)
     same = ((b % 256) % JB == a) & (b % 256 < 216)
     mixed[216:256, :] = jnp.zeros((40, SEC * 96), BF)
     last = None
     for n, r in enumerate(ORDER):
-        rows = [
-            jnp.where(same, weights[r * DD + l:r * DD + l + 1, :], 0.0).astype(BF) for l in ORDER
-        ]
+        rows = [jnp.where(same, wide[r * DD + l:r * DD + l + 1, :], 0.0).astype(BF) for l in ORDER]
         last = nt(jnp.concatenate(rows, axis=0), at[...]).astype(BF)
         if n < SEC:
             mixed[0:216, n * 96:(n + 1) * 96] = last
@@ -222,25 +213,32 @@
     for p, (host, spot) in enumerate(IN_PLACES):
         sector = jnp.where(lane // XB == spot * SEC + host, p, sector)
     for v in range(SEC):
-        spread[v * 256:(v + 1) * 256, :] = jnp.where(sector == v, mixed[...], zero)
+        spread[v * 256:(v + 1) * 256, :] = jnp.where(sector == v, mixed[...], jnp.zeros((), BF))
     for n in range(3):
         cut = slice(n * 256, (n + 1) * 256)
-        out[:, cut] = nn(lower_v[...], spread[:, cut]).astype(BF)
+        total = nn(lower_v[...], spread[:, cut])
+        for g in range(NY):
+            ours[g, :, cut] = total[g * 48:g * 48 + 24]
+            theirs[g, :, cut] = total[g * 48 + 24:(g + 1) * 48].astype(BF)
 
 
 def main(site, lb, u):
     return pl.pallas_call(
         main_kernel,
-        out_shape=jax.ShapeDtypeStruct((CAP, SEC * 96), BF),
+        out_shape=(
+            jax.ShapeDtypeStruct((NY, JB, SEC * 96), F32),
+            jax.ShapeDtypeStruct((NY, JB, SEC * 96), BF),
+        ),
         in_specs=[VMEM] * 3,
-        out_specs=VMEM,
+        out_specs=(VMEM, VMEM),
         scratch_shapes=[
             pltpu.VMEM((SEC, CAP, 256), BF),
             pltpu.VMEM((CAP, SEC * 256), BF),
-            pltpu.VMEM((SEC * 128, 256), BF),
+            pltpu.VMEM((96, DD * 256), F32),
             pltpu.VMEM((96, DD * 256), BF),
             pltpu.VMEM((256, SEC * 96), BF),
             pltpu.VMEM((SEC * 256, SEC * 96), BF),
+            pltpu.VMEM((81, DD * 256), F32),
         ],
         compiler_params=PARAMS,
         name="main",
@@ -249,7 +247,7 @@
 
 def finish_kernel(terms, out, stacked):
     total = terms[0].astype(F32)
-    for z in range(1, N_LO):
+    for z in range(1, N_LO // 2):
         total = total + terms[z].astype(F32)
     for n in range(SEC):
         r = ORDER[n]
@@ -277,28 +275,32 @@
     )(terms)
 
 
+Z_GROUPS = [[2 * z + core for z in range(N_LO // 2)] for core in range(2)]
 X_GROUPS = [[y * NX + x for x in range(NX)] for y in range(NY)]
 Y_GROUPS = [[y * NX + x for y in range(NY)] for x in range(NX)]
 
 
 def local(sector_sizes, left, upper_edge, lower_edge, site_block):
     charges = jnp.array(CHARGE, dtype=jnp.int32)
-    place = jnp.stack([lax.axis_index("up"), lax.axis_index("lo")]).astype(jnp.int32)
+    lb, u = prepare(sector_sizes, left, upper_edge, lower_edge)
+    site_block, lb = lax.optimization_barrier((site_block, lb))
     even = (
         charges[:, None, None, None] + charges[None, None, :, None]
         == charges[None, :, None, None] + charges[None, None, None, :]
     )
     site = jnp.where(even, site_block, jnp.float32(0.0))
     site = site.transpose(2, 3, 0, 1).reshape(81, 81)
-    lb, u = prepare(sector_sizes, place, left, upper_edge, lower_edge)
     line = lax.all_to_all(lb, "up", 0, 0, axis_index_groups=Y_GROUPS)
     line, u, site = lax.optimization_barrier((line, u, site))
     whole = lax.all_to_all(
         jnp.broadcast_to(line, (NX,) + line.shape), "up", 0, 0, axis_index_groups=X_GROUPS
     )
     u = lax.all_gather(u, "lo", axis=0)
-    terms = main(site, whole, u)
-    terms = lax.all_to_all(terms.reshape(N_LO, JB, SEC * 96), "lo", 0, 0)
+    ours, theirs = main(site, whole, u)
+    swap = [(n, n + 1 - 2 * (n % 2)) for n in range(N_LO)]
+    theirs = lax.ppermute(theirs, "lo", swap)
+    terms = (ours + theirs.astype(F32)).astype(BF)
+    terms = lax.all_to_all(terms, "lo", 0, 0, axis_index_groups=Z_GROUPS)
     return finish(terms)
 
 

time: 111 us -> 100 us (0.901)
  blocking collectives: 58.3 us -> 47.9 us
  Pallas kernels: 16.1 us -> 11.5 us
  starting transfers between devices: 14.7 us -> 18.3 us
  waiting for transfers between devices: 14.7 us -> 17.9 us
  local copies, waits for them, and re-layouts: 4.09 us -> 2.05 us
    all_to_all x1, blocking collectives: 31 us -> 22 us  [local(): terms = lax.all_to_all(terms, 'lo', 0, 0, axis_index_groups=Z_GROUPS)]
    ppermute x0 -> x1, starting transfers between devices: none -> 3.57 us  [local(): theirs = lax.ppermute(theirs, 'lo', swap)]
    pallas_call x1, Pallas kernels: 11.1 us -> 7.65 us  [main(): pl.pallas_call(main_kernel, out_shape=(jax.ShapeDtypeStruct((NY, JB, SEC...]
    unnamed x4 -> x2, local copies, waits for them, and re-layouts: 1.41 us -> 0.01 us
    all_gather x1, blocking collectives: 27.3 us -> 25.9 us  [local(): u = lax.all_gather(u, 'lo', axis=0)]
    all_to_all x1, waiting for transfers between devices: 1.13 us -> 2.52 us  [local(): lax.all_to_all(jnp.broadcast_to(line, (NX,) + line.shape), 'up', 0, 0, ax...]
    ppermute x0 -> x1, waiting for transfers between devices: none -> 1.19 us  [local(): theirs = lax.ppermute(theirs, 'lo', swap)]
  transfers between devices with their start and end apart: 2 -> 3, of which waited for: 2 -> 3; matrix products, arithmetic and copies ran while one was open for 3% -> 2% of each run, Pallas kernels for 0% -> 0%
where the time goes in v2:
time: 100 us; the launch traced here: 99.8 us
  blocking collectives  47.9 us (48%)
  starting transfers between devices  18.3 us (18%)
  waiting for transfers between devices  17.9 us (18%)
  Pallas kernels  11.5 us (12%)
  other arithmetic  2.07 us (2%)
  local copies, waits for them, and re-layouts  2.05 us (2%)
    all_gather x1, blocking collectives, local(): u = lax.all_gather(u, 'lo', axis=0)  25.9 us
    all_to_all x1, blocking collectives, local(): terms = lax.all_to_all(terms, 'lo', 0, 0, axis_index_groups=Z_GROUPS)  22 us
    all_to_all x1, waiting for transfers between devices, local(): line = lax.all_to_all(lb, 'up', 0, 0, axis_index_groups=Y_GROUPS)  14.2 us
    pallas_call x1, Pallas kernels, main(): pl.pallas_call(main_kernel, out_shape=(jax.ShapeDtypeStruct((NY, JB, SEC...  7.65 us
    all_to_all x1, starting transfers between devices, local(): line = lax.all_to_all(lb, 'up', 0, 0, axis_index_groups=Y_GROUPS)  7.65 us
    all_to_all x1, starting transfers between devices, local(): lax.all_to_all(jnp.broadcast_to(line, (NX,) + line.shape), 'up', 0, 0, ax...  7.04 us
    ppermute x1, starting transfers between devices, local(): theirs = lax.ppermute(theirs, 'lo', swap)  3.57 us
    pallas_call x1, Pallas kernels, prepare(): pl.pallas_call(prepare_kernel, out_shape=(jax.ShapeDtypeStruct((NY, 288,...  3 us
  transfers between devices with their start and end apart: 3, of which 3 were waited for; matrix products, arithmetic and copies ran while one was open for 2% of the time, Pallas kernels for 0%

profile of v2, /device:TPU:1, one launch (start us, length us, event | category | flops | bytes accessed | tf_op | source)
XLA Modules:
  0.0 99.8 jit_solution(10192157637589536830)
XLA Ops:
  0.0 3.0 %prepare.1 = (bf16[8,288,128]{2,1,0:T(8,128)(2,1)}, bf16[192,128]{1,0:T(8,128)(2,1)}) custom-call(s32[8]{0:T(128)} %sizes.1, bf16[9,24,96]{2,1,0:T(8,128)(2,1)} %left.1, bf16[9,12,192]{2,1,0:T(8,128)(2,1)} %upper.1, bf16[9,12,192]{2,1,0:T(8,128)(2,1)} %lower.1), custom_call_target="tpu_custom_call" | custom-call | tf_op jit(solution)/shard_map/prepare/pallas_call | solution.py:130
  3.0 7.6 %all-to-all-start = ((bf16[8,288,128]{2,1,0:T(8,128)(2,1)}), bf16[8,288,128]{2,1,0:T(8,128)(2,1)S(1)}, u32[]{:S(2)}, u32[]{:S(2)}) async-start(bf16[8,288,128]{2,1,0:T(8,128)(2,1)} %get-tuple-element.15), calls=%async_computation | async-start | bytes 1179648 | tf_op jit(solution)/shard_map/all_to_all | solution.py:293
  10.7 0.8 broadcast_add_fusion
  11.5 1.2 %select_bitcast_fusion = f32[9,9,9,9]{1,0,3,2:T(8,128)S(1)} fusion(f32[9,9,9,9]{3,2,1,0:T(8,128)} %param.10, s32[9,9]{1,0:T(8,128)S(1)} %broadcast_add_fusion), kind=kLoop, calls=%fused_computation | loop fusion | flops 13122 | bytes 52812 | tf_op jit(solution)/shard_map/transpose | solution.py:292
  12.7 0.2 reshape.67
  12.9 0.1 copy.8.site
  13.0 14.2 %all-to-all-done = bf16[8,288,128]{2,1,0:T(8,128)(2,1)S(1)} async-done(((bf16[8,288,128]{2,1,0:T(8,128)(2,1)}), bf16[8,288,128]{2,1,0:T(8,128)(2,1)S(1)}, u32[]{:S(2)}, u32[]{:S(2)}) %all-to-all-start) | async-done | bytes 589856 | tf_op jit(solution)/shard_map/all_to_all | solution.py:293
  27.1 1.7 %broadcast_in_dim.12 = bf16[4,8,288,128]{3,2,1,0:T(8,128)(2,1)} broadcast(bf16[8,288,128]{2,1,0:T(8,128)(2,1)S(1)} %all-to-all-done), dimensions={1,2,3} | broadcast | bytes 2949120 | tf_op jit(solution)/shard_map/broadcast_in_dim | solution.py:296
  28.9 0.0 copy-start
  28.9 7.0 %all-to-all-start.1 = ((bf16[4,8,288,128]{3,2,1,0:T(8,128)(2,1)}), bf16[4,8,288,128]{3,2,1,0:T(8,128)(2,1)S(1)}, u32[]{:S(2)}, u32[]{:S(2)}) async-start(bf16[4,8,288,128]{3,2,1,0:T(8,128)(2,1)} %broadcast_in_dim.12), calls=%async_computation.1 | async-start | bytes 4718592 | tf_op jit(solution)/shard_map/all_to_all | solution.py:295
  35.9 0.0 copy-done
  35.9 25.9 %all-gather = bf16[3072,128]{1,0:T(8,128)(2,1)S(1)} all-gather(bf16[192,128]{1,0:T(8,128)(2,1)S(1)} %copy-done), channel_id=2, replica_groups=mesh['up'=32,'lo'=16] {'lo'}, dimensions={0}, use_global_device_ids=true | all-gather | bytes 835584 | tf_op jit(solution)/shard_map/all_gather | solution.py:298
  61.8 2.5 %all-to-all-done.1.lb = bf16[4,8,288,128]{3,2,1,0:T(8,128)(2,1)S(1)} async-done(((bf16[4,8,288,128]{3,2,1,0:T(8,128)(2,1)}), bf16[4,8,288,128]{3,2,1,0:T(8,128)(2,1)S(1)}, u32[]{:S(2)}, u32[]{:S(2)}) %all-to-all-start.1) | async-done | bytes 2359328 | tf_op jit(solution)/shard_map/all_to_all | solution.py:295
  64.3 7.7 %main.1 = (f32[8,24,768]{2,1,0:T(8,128)S(1)}, bf16[8,24,768]{2,1,0:T(8,128)(2,1)S(1)}) custom-call(f32[81,81]{1,0:T(8,128)S(1)} %copy.8.site, bf16[4,8,288,128]{3,2,1,0:T(8,128)(2,1)S(1)} %all-to-all-done.1.lb, bf16[16,192,128]{2,1,0:T(8,128)(2,1)S(1)} %bitcast.5), custom_call_target="tpu_custom_call" | custom-call | tf_op jit(solution)/shard_map/main/pallas_call | solution.py:226
  72.0 3.6 %collective-permute-start = (bf16[8,24,768]{2,1,0:T(8,128)(2,1)S(1)}, bf16[8,24,768]{2,1,0:T(8,128)(2,1)S(1)}, u32[]{:S(2)}, u32[]{:S(2)}) collective-permute-start(bf16[8,24,768]{2,1,0:T(8,128)(2,1)S(1)} %get-tuple-element.22), channel_id=1, source_target_pairs={{0,1},{1,0},{2,3},{3,2},{4,5},{5,4},{6,7},{7,6},{8,9},{9,8},{10,11... | collective-permute-start | bytes 884744 | tf_op jit(solution)/shard_map/ppermute | solution.py:301
  75.6 1.2 %collective-permute-done = bf16[8,24,768]{2,1,0:T(8,128)(2,1)S(1)} collective-permute-done((bf16[8,24,768]{2,1,0:T(8,128)(2,1)S(1)}, bf16[8,24,768]{2,1,0:T(8,128)(2,1)S(1)}, u32[]{:S(2)}, u32[]{:S(2)}) %collective-permute-start) | collective-permute-done | bytes 294944 | tf_op jit(solution)/shard_map/ppermute | solution.py:301
  76.8 0.1 add_convert_fusion
  76.8 22.0 %all_to_all.15.terms = bf16[8,24,768]{2,1,0:T(8,128)(2,1)S(1)} all-to-all(bf16[8,24,768]{2,1,0:T(8,128)(2,1)S(1)} %add_convert_fusion), channel_id=1, replica_groups={{0,2,4,6,8,10,12,14},{1,3,5,7,9,11,13,15},{16,18,20,22,24,26,28,30},{17..., dimensions={0} | all-to-all | bytes 589824 | tf_op jit(solution)/shard_map/all_to_all | solution.py:303
  98.9 0.9 finish.1
Async XLA Ops:
  3.0 24.1 %all-to-all-start = ((bf16[8,288,128]{2,1,0:T(8,128)(2,1)}), bf16[8,288,128]{2,1,0:T(8,128)(2,1)S(1)}, u32[]{:S(2)}, u32[]{:S(2)}) async-start(bf16[8,288,128]{2,1,0:T(8,128)(2,1)} %get-tuple-element.15), calls=%async_computation | async-start | bytes 1179648 | tf_op jit(solution)/shard_map/all_to_all | solution.py:293
  28.9 7.0 %copy-start = (bf16[192,128]{1,0:T(8,128)(2,1)S(1)}, bf16[192,128]{1,0:T(8,128)(2,1)}, u32[]{:S(2)}) copy-start(bf16[192,128]{1,0:T(8,128)(2,1)} %get-tuple-element.20) | copy-start | bytes 147460
  28.9 35.5 %all-to-all-start.1 = ((bf16[4,8,288,128]{3,2,1,0:T(8,128)(2,1)}), bf16[4,8,288,128]{3,2,1,0:T(8,128)(2,1)S(1)}, u32[]{:S(2)}, u32[]{:S(2)}) async-start(bf16[4,8,288,128]{3,2,1,0:T(8,128)(2,1)} %broadcast_in_dim.12), calls=%async_computation.1 | async-start | bytes 4718592 | tf_op jit(solution)/shard_map/all_to_all | solution.py:295
  72.0 4.8 %collective-permute-start = (bf16[8,24,768]{2,1,0:T(8,128)(2,1)S(1)}, bf16[8,24,768]{2,1,0:T(8,128)(2,1)S(1)}, u32[]{:S(2)}, u32[]{:S(2)}) collective-permute-start(bf16[8,24,768]{2,1,0:T(8,128)(2,1)S(1)} %get-tuple-element.22), channel_id=1, source_target_pairs={{0,1},{1,0},{2,3},{3,2},{4,5},{5,4},{6,7},{7,6},{8,9},{9,8},{10,11... | collective-permute-start | bytes 884744 | tf_op jit(solution)/shard_map/ppermute | solution.py:301

commit v3 on v2

--- a/solution.py
+++ b/solution.py
@@ -116,13 +116,11 @@
     pack[1] = grid[:, 0:192]
     for v, (host, at) in enumerate(OUT_PLACES):
         pack[1, host * XB:(host + 1) * XB, at * JB:(at + 1) * JB] = grid[v * XB:(v + 1) * XB, 192:216]
-    ours = pack[0].astype(BF)
-    theirs = pack[1].astype(BF)
     for n in range(NY):
-        lb_out[n, 0:96, :] = ours[:, 0:128]
-        lb_out[n, 96:192, :] = theirs[:, 0:128]
-        lb_out[n, 192:288, 0:64] = ours[:, 128:192]
-        lb_out[n, 192:288, 64:128] = theirs[:, 128:192]
+        for side in range(2):
+            lb_out[n, side, 0:96, :] = pack[side, :, 0:128].astype(BF)
+            lb_out[n, side, 96:144, 0:64] = pack[side, 0:48, 128:192].astype(BF)
+            lb_out[n, side, 96:144, 64:128] = pack[side, 48:96, 128:192].astype(BF)
     u_out[...] = edge
 
 
@@ -130,7 +128,7 @@
     return pl.pallas_call(
         prepare_kernel,
         out_shape=(
-            jax.ShapeDtypeStruct((NY, 288, 128), BF),
+            jax.ShapeDtypeStruct((NY, 2, 144, 128), BF),
             jax.ShapeDtypeStruct((192, 128), BF),
         ),
         in_specs=[SMEM, VMEM, VMEM, VMEM],
@@ -148,8 +146,17 @@
 
 def regrouping(turn):
     a, b = iota((384, 384), 0), iota((384, 384), 1)
-    x = ((a % 48) // XB + turn) % NX
-    return one_hot(b == x * 96 + (a // 48) * XB + a % XB)
+    d = ((a % 48) // XB + turn + NX - lax.axis_index("up") % NX) % NX
+    return one_hot(b == d * 96 + (a // 48) * XB + a % XB)
+
+
+def regrouped(regroup, pieces, g):
+    lines = [piece[g] for piece in pieces]
+    near = jnp.concatenate([line[0:96, :] for line in lines], axis=0)
+    far = jnp.concatenate(
+        [line[96:144, 64 * h:64 * (h + 1)] for line in lines for h in range(2)], axis=0
+    )
+    return nn(regroup, jnp.concatenate([near, far], axis=1)).astype(BF)
 
 
 def spread_out(part, charge, hosts, sector):
@@ -162,25 +169,16 @@
     return rows, part[host * 48:(host + 1) * 48, spot * JB:(spot + 1) * JB]
 
 
-def main_kernel(site, lb, u, ours, theirs, left_q, lower_v, moved, at, mixed, spread, wide):
-    regroup_left = regrouping(0)
-    regroup_lower = regrouping(2 * lax.rem(lax.axis_index("lo"), 2))
+def mix_kernel(site, u, own, right, far, left, mixed, left_q, moved, at, wide):
+    regroup = regrouping(0)
     left_q[...] = jnp.zeros(left_q.shape, BF)
-    lower_v[...] = jnp.zeros(lower_v.shape, BF)
     moved[...] = jnp.zeros(moved.shape, F32)
     for g in range(NY):
-        near, other, far = [lb[:, g, 96 * n:96 * (n + 1), :].reshape(384, 128) for n in range(3)]
-        rows = slice(g * 48, (g + 1) * 48)
-        part = nn(regroup_left, jnp.concatenate([near, far[:, 0:64]], axis=1)).astype(BF)
+        part = regrouped(regroup, (own, right, far, left), g)
         for q in range(SEC):
-            own, last = spread_out(part, CHARGE, IN_PLACES, q)
-            left_q[q, rows, 0:192] = own
-            left_q[q, rows, 192:216] = last
-        part = nn(regroup_lower, jnp.concatenate([other, far[:, 64:128]], axis=1)).astype(BF)
-        for v in range(SEC):
-            own, last = spread_out(part, [-c for c in CHARGE], OUT_PLACES, v)
-            lower_v[rows, v * 256:v * 256 + 192] = own
-            lower_v[rows, v * 256 + 192:v * 256 + 216] = last
+            rows, last = spread_out(part, CHARGE, IN_PLACES, q)
+            left_q[q, g * 48:(g + 1) * 48, 0:192] = rows
+            left_q[q, g * 48:(g + 1) * 48, 192:216] = last
     for q in range(SEC):
         columns = u[:, q * JB:(q + 1) * JB, :].reshape(CAP, 128)
         image = tn(columns, left_q[q])
@@ -206,6 +204,35 @@
     for p, (host, spot) in enumerate(IN_PLACES):
         start = spot * 96 + host * XB
         mixed[0:216, start:start + XB] = last[:, p * XB:(p + 1) * XB]
+
+
+def mix(site, u, pieces):
+    return pl.pallas_call(
+        mix_kernel,
+        out_shape=jax.ShapeDtypeStruct((256, SEC * 96), BF),
+        in_specs=[VMEM] * 6,
+        out_specs=VMEM,
+        scratch_shapes=[
+            pltpu.VMEM((SEC, CAP, 256), BF),
+            pltpu.VMEM((96, DD * 256), F32),
+            pltpu.VMEM((96, DD * 256), BF),
+            pltpu.VMEM((81, DD * 256), F32),
+        ],
+        compiler_params=PARAMS,
+        cost_estimate=pl.CostEstimate(flops=6_000_000_000, bytes_accessed=3_000_000, transcendentals=0),
+        name="mix",
+    )(site, u, *pieces)
+
+
+def lower_kernel(mixed, own, right, far, left, ours, theirs, lower_v, spread):
+    regroup = regrouping(2 * lax.rem(lax.axis_index("lo"), 2))
+    lower_v[...] = jnp.zeros(lower_v.shape, BF)
+    for g in range(NY):
+        part = regrouped(regroup, (own, right, far, left), g)
+        for v in range(SEC):
+            rows, last = spread_out(part, [-c for c in CHARGE], OUT_PLACES, v)
+            lower_v[g * 48:(g + 1) * 48, v * 256:v * 256 + 192] = rows
+            lower_v[g * 48:(g + 1) * 48, v * 256 + 192:v * 256 + 216] = last
     lane = iota((1, SEC * 96), 1)
     sector = (lane % 96) // XB
     for n in range(SEC):
@@ -222,27 +249,22 @@
             theirs[g, :, cut] = total[g * 48 + 24:(g + 1) * 48].astype(BF)
 
 
-def main(site, lb, u):
+def contract_lower(mixed, pieces):
     return pl.pallas_call(
-        main_kernel,
+        lower_kernel,
         out_shape=(
             jax.ShapeDtypeStruct((NY, JB, SEC * 96), F32),
             jax.ShapeDtypeStruct((NY, JB, SEC * 96), BF),
         ),
-        in_specs=[VMEM] * 3,
+        in_specs=[VMEM] * 5,
         out_specs=(VMEM, VMEM),
         scratch_shapes=[
-            pltpu.VMEM((SEC, CAP, 256), BF),
             pltpu.VMEM((CAP, SEC * 256), BF),
-            pltpu.VMEM((96, DD * 256), F32),
-            pltpu.VMEM((96, DD * 256), BF),
-            pltpu.VMEM((256, SEC * 96), BF),
             pltpu.VMEM((SEC * 256, SEC * 96), BF),
-            pltpu.VMEM((81, DD * 256), F32),
         ],
         compiler_params=PARAMS,
-        name="main",
-    )(site, lb, u)
+        name="lower",
+    )(mixed, *pieces)
 
 
 def finish_kernel(terms, out, stacked):
@@ -276,8 +298,12 @@
 
 
 Z_GROUPS = [[2 * z + core for z in range(N_LO // 2)] for core in range(2)]
-X_GROUPS = [[y * NX + x for x in range(NX)] for y in range(NY)]
 Y_GROUPS = [[y * NX + x for y in range(NY)] for x in range(NX)]
+
+
+def from_x(value, d):
+    pairs = [(y * NX + x, y * NX + (x - d) % NX) for y in range(NY) for x in range(NX)]
+    return lax.ppermute(value, "up", pairs)
 
 
 def local(sector_sizes, left, upper_edge, lower_edge, site_block):
@@ -291,12 +317,14 @@
     site = jnp.where(even, site_block, jnp.float32(0.0))
     site = site.transpose(2, 3, 0, 1).reshape(81, 81)
     line = lax.all_to_all(lb, "up", 0, 0, axis_index_groups=Y_GROUPS)
+    u = lax.all_gather(u, "lo", axis=0)
     line, u, site = lax.optimization_barrier((line, u, site))
-    whole = lax.all_to_all(
-        jnp.broadcast_to(line, (NX,) + line.shape), "up", 0, 0, axis_index_groups=X_GROUPS
-    )
-    u = lax.all_gather(u, "lo", axis=0)
-    ours, theirs = main(site, whole, u)
+    left, lower = line[:, 0], line[:, 1]
+    left_right, left_left = from_x(left, 1), from_x(left, -1)
+    lower_right, lower_left = from_x(lower, 1), from_x(lower, -1)
+    left_far, lower_far = from_x(left_right, 1), from_x(lower_left, -1)
+    mixed = mix(site, u, (left, left_right, left_far, left_left))
+    ours, theirs = contract_lower(mixed, (lower, lower_right, lower_far, lower_left))
     swap = [(n, n + 1 - 2 * (n % 2)) for n in range(N_LO)]
     theirs = lax.ppermute(theirs, "lo", swap)
     terms = (ours + theirs.astype(F32)).astype(BF)

time: 100 us -> 91.7 us (0.917)
  waiting for transfers between devices: 17.9 us -> 5.05 us
  starting transfers between devices: 18.3 us -> 30.8 us
  blocking collectives: 47.9 us -> 41.1 us
  other arithmetic: 2.07 us -> 0.24 us
  local copies, waits for them, and re-layouts: 2.05 us -> 1.04 us
  Pallas kernels: 11.5 us -> 12.5 us
    ppermute x0 -> x6, starting transfers between devices: none -> 19 us  [from_x(): return lax.ppermute(value, 'up', pairs)]
    all_to_all x1, waiting for transfers between devices: 14.2 us -> 0.01 us  [local(): line = lax.all_to_all(lb, 'up', 0, 0, axis_index_groups=Y_GROUPS)]
    all_to_all x1 -> x0, starting transfers between devices: 7.04 us -> none  [local(): lax.all_to_all(jnp.broadcast_to(line, (NX,) + line.shape), 'up', 0, 0, ax...]
    all_to_all x1, blocking collectives: 22 us -> 15.1 us  [local(): terms = lax.all_to_all(terms, 'lo', 0, 0, axis_index_groups=Z_GROUPS)]
    ppermute x0 -> x6, waiting for transfers between devices: none -> 3.87 us  [from_x(): return lax.ppermute(value, 'up', pairs)]
    all_to_all x1 -> x0, waiting for transfers between devices: 2.52 us -> none  [local(): lax.all_to_all(jnp.broadcast_to(line, (NX,) + line.shape), 'up', 0, 0, ax...]
    broadcast_in_dim x1 -> x0, local copies, waits for them, and re-layouts: 1.75 us -> none  [local(): jnp.broadcast_to(line, (NX,) + line.shape)]
    transpose x1, other arithmetic: 1.2 us -> 0.11 us  [local(): site = site.transpose(2, 3, 0, 1).reshape(81, 81)]
  transfers between devices with their start and end apart: 3 -> 8, of which waited for: 3 -> 5; matrix products, arithmetic and copies ran while one was open for 2% -> 1% of each run, Pallas kernels for 0% -> 6%
where the time goes in v3:
time: 91.7 us; the launch traced here: 90.9 us
  blocking collectives  41.1 us (45%)
  starting transfers between devices  30.8 us (34%)
  Pallas kernels  12.5 us (14%)
  waiting for transfers between devices  5.05 us (6%)
  local copies, waits for them, and re-layouts  1.04 us (1%)
    all_gather x1, blocking collectives, local(): u = lax.all_gather(u, 'lo', axis=0)  26.1 us
    ppermute x6, starting transfers between devices, from_x(): return lax.ppermute(value, 'up', pairs)  19 us
    all_to_all x1, blocking collectives, local(): terms = lax.all_to_all(terms, 'lo', 0, 0, axis_index_groups=Z_GROUPS)  15.1 us
    all_to_all x1, starting transfers between devices, local(): line = lax.all_to_all(lb, 'up', 0, 0, axis_index_groups=Y_GROUPS)  7.78 us
    pallas_call x1, Pallas kernels, mix(): pl.pallas_call(mix_kernel, out_shape=jax.ShapeDtypeStruct((256, SEC * 96)...  5.33 us
    ppermute x1, starting transfers between devices, local(): theirs = lax.ppermute(theirs, 'lo', swap)  4.07 us
    ppermute x6, waiting for transfers between devices, from_x(): return lax.ppermute(value, 'up', pairs)  3.87 us
    pallas_call x1, Pallas kernels, contract_lower(): pl.pallas_call(lower_kernel, out_shape=(jax.ShapeDtypeStruct((NY, JB, SEC...  3.23 us
  transfers between devices with their start and end apart: 8, of which 5 were waited for; matrix products, arithmetic and copies ran while one was open for 1% of the time, Pallas kernels for 6%

profile of v3, /device:TPU:1, one launch (start us, length us, event | category | flops | bytes accessed | tf_op | source)
XLA Modules:
  0.0 90.9 jit_solution(18159989582515391043)
XLA Ops:
  0.0 0.0 copy-start
  0.0 3.0 %prepare.1 = (bf16[8,2,144,128]{3,2,1,0:T(8,128)(2,1)}, bf16[192,128]{1,0:T(8,128)(2,1)}) custom-call(s32[8]{0:T(128)} %sizes.1, bf16[9,24,96]{2,1,0:T(8,128)(2,1)} %left.1, bf16[9,12,192]{2,1,0:T(8,128)(2,1)} %upper.1, bf16[9,12,192]{2,1,0:T(8,128)(2,1)} %lower.2), custom_call_target="tpu_custom_call" | custom-call | tf_op jit(solution)/shard_map/prepare/pallas_call | solution.py:128
  3.0 0.0 copy-start.2
  3.0 7.8 %all-to-all-start = ((bf16[8,2,144,128]{3,2,1,0:T(8,128)(2,1)}), bf16[8,2,144,128]{3,2,1,0:T(8,128)(2,1)S(1)}, u32[]{:S(2)}, u32[]{:S(2)}) async-start(bf16[8,2,144,128]{3,2,1,0:T(8,128)(2,1)} %get-tuple-element.15), calls=%async_computation | async-start | bytes 1179648 | tf_op jit(solution)/shard_map/all_to_all | solution.py:319
  10.8 0.0 copy-done.2
  10.8 0.1 broadcast_add_fusion
  10.9 0.0 copy-done
  10.9 0.1 select_bitcast_fusion
  11.0 0.2 reshape.67
  11.2 0.1 copy.12.site
  11.3 0.7 copy-done.1
  12.0 26.1 %all-gather = bf16[3072,128]{1,0:T(8,128)(2,1)S(1)} all-gather(bf16[192,128]{1,0:T(8,128)(2,1)S(1)} %copy-done.1), channel_id=2, replica_groups=mesh['up'=32,'lo'=16] {'lo'}, dimensions={0}, use_global_device_ids=true | all-gather | bytes 835584 | tf_op jit(solution)/shard_map/all_gather | solution.py:320
  38.1 0.0 all-to-all-done
  38.2 4.4 %collective-permute-start = (bf16[8,144,128]{2,1,0:T(8,128)(2,1)S(1)}, bf16[8,144,128]{2,1,0:T(8,128)(2,1)S(1)}, u32[]{:S(2)}, u32[]{:S(2)}) collective-permute-start(bf16[8,144,128]{2,1,0:T(8,128)(2,1)S(1)} %get-tuple-element.24.own), channel_id=1, source_target_pairs={{0,48},{16,0},{32,16},{48,32},{64,112},{80,64},{96,80},{112,96},{1... | collective-permute-start | bytes 884744 | tf_op jit(solution)/shard_map/ppermute | solution.py:306
  42.5 1.9 %collective-permute-start.4 = (bf16[8,144,128]{2,1,0:T(8,128)(2,1)S(1)}, bf16[8,144,128]{2,1,0:T(8,128)(2,1)S(1)}, u32[]{:S(2)}, u32[]{:S(2)}) collective-permute-start(bf16[8,144,128]{2,1,0:T(8,128)(2,1)S(1)} %get-tuple-element.23.own), channel_id=1, source_target_pairs={{0,16},{16,32},{32,48},{48,0},{64,80},{80,96},{96,112},{112,64},{1... | collective-permute-start | bytes 884744 | tf_op jit(solution)/shard_map/ppermute | solution.py:306
  44.5 2.1 %collective-permute-start.2 = (bf16[8,144,128]{2,1,0:T(8,128)(2,1)S(1)}, bf16[8,144,128]{2,1,0:T(8,128)(2,1)S(1)}, u32[]{:S(2)}, u32[]{:S(2)}) collective-permute-start(bf16[8,144,128]{2,1,0:T(8,128)(2,1)S(1)} %get-tuple-element.24.own), channel_id=1, source_target_pairs={{0,16},{16,32},{32,48},{48,0},{64,80},{80,96},{96,112},{112,64},{1... | collective-permute-start | bytes 884744 | tf_op jit(solution)/shard_map/ppermute | solution.py:306
  46.6 2.2 %collective-permute-done.right = bf16[8,144,128]{2,1,0:T(8,128)(2,1)S(1)} collective-permute-done((bf16[8,144,128]{2,1,0:T(8,128)(2,1)S(1)}, bf16[8,144,128]{2,1,0:T(8,128)(2,1)S(1)}, u32[]{:S(2)}, u32[]{:S(2)}) %collective-permute-start) | collective-permute-done | bytes 294944 | tf_op jit(solution)/shard_map/ppermute | solution.py:306
  48.8 5.3 %collective-permute-start.1 = (bf16[8,144,128]{2,1,0:T(8,128)(2,1)S(1)}, bf16[8,144,128]{2,1,0:T(8,128)(2,1)S(1)}, u32[]{:S(2)}, u32[]{:S(2)}) collective-permute-start(bf16[8,144,128]{2,1,0:T(8,128)(2,1)S(1)} %collective-permute-done.right), channel_id=1, source_target_pairs={{0,48},{16,0},{32,16},{48,32},{64,112},{80,64},{96,80},{112,96},{1... | collective-permute-start | bytes 884744 | tf_op jit(solution)/shard_map/ppermute | solution.py:306
  54.1 1.9 %collective-permute-start.3 = (bf16[8,144,128]{2,1,0:T(8,128)(2,1)S(1)}, bf16[8,144,128]{2,1,0:T(8,128)(2,1)S(1)}, u32[]{:S(2)}, u32[]{:S(2)}) collective-permute-start(bf16[8,144,128]{2,1,0:T(8,128)(2,1)S(1)} %get-tuple-element.23.own), channel_id=1, source_target_pairs={{0,48},{16,0},{32,16},{48,32},{64,112},{80,64},{96,80},{112,96},{1... | collective-permute-start | bytes 884744 | tf_op jit(solution)/shard_map/ppermute | solution.py:306
  56.0 0.0 collective-permute-done.4.left
  56.0 3.4 %collective-permute-start.5 = (bf16[8,144,128]{2,1,0:T(8,128)(2,1)S(1)}, bf16[8,144,128]{2,1,0:T(8,128)(2,1)S(1)}, u32[]{:S(2)}, u32[]{:S(2)}) collective-permute-start(bf16[8,144,128]{2,1,0:T(8,128)(2,1)S(1)} %collective-permute-done.4.left), channel_id=1, source_target_pairs={{0,16},{16,32},{32,48},{48,0},{64,80},{80,96},{96,112},{112,64},{1... | collective-permute-start | bytes 884744 | tf_op jit(solution)/shard_map/ppermute | solution.py:306
  59.4 0.7 collective-permute-done.2.left
  60.1 0.0 collective-permute-done.1.far
  60.1 5.3 %mix.1.mixed = bf16[256,768]{1,0:T(8,128)(2,1)S(1)} custom-call(f32[81,81]{1,0:T(8,128)S(1)} %copy.12.site, bf16[16,192,128]{2,1,0:T(8,128)(2,1)S(1)} %bitcast.9, bf16[8,144,128]{2,1,0:T(8,128)(2,1)S(1)} %get-tuple-element.24.own, bf16[8,144,128]{2,1,0:T(8,128)(2,1)S(1)} %collective-permute-done.right, bf16[8,144,128]{2,1,0:T(8,128)(2,1)S(1)} %collective-permute-done.1.far, ...), custom_call_target="tpu_custom_call" | custom-call | flops 6000000000 | bytes 3000000 | tf_op jit(solution)/shard_map/mix/pallas_call | solution.py:210
  65.4 0.3 collective-permute-done.3.right
  65.7 0.7 collective-permute-done.5.far
  66.4 3.2 %lower.3 = (f32[8,24,768]{2,1,0:T(8,128)S(1)}, bf16[8,24,768]{2,1,0:T(8,128)(2,1)S(1)}) custom-call(bf16[256,768]{1,0:T(8,128)(2,1)S(1)} %mix.1.mixed, bf16[8,144,128]{2,1,0:T(8,128)(2,1)S(1)} %get-tuple-element.23.own, bf16[8,144,128]{2,1,0:T(8,128)(2,1)S(1)} %collective-permute-done.3.right, bf16[8,144,128]{2,1,0:T(8,128)(2,1)S(1)} %collective-permute-done.5.far, ...), custom_call_target="tpu_custom_call" | custom-call | tf_op jit(solution)/shard_map/lower/pallas_call | solution.py:253
  69.6 4.1 %collective-permute-start.6 = (bf16[8,24,768]{2,1,0:T(8,128)(2,1)S(1)}, bf16[8,24,768]{2,1,0:T(8,128)(2,1)S(1)}, u32[]{:S(2)}, u32[]{:S(2)}) collective-permute-start(bf16[8,24,768]{2,1,0:T(8,128)(2,1)S(1)} %get-tuple-element.22), channel_id=1, source_target_pairs={{0,1},{1,0},{2,3},{3,2},{4,5},{5,4},{6,7},{7,6},{8,9},{9,8},{10,11... | collective-permute-start | bytes 884744 | tf_op jit(solution)/shard_map/ppermute | solution.py:329
  73.7 1.2 %collective-permute-done.6 = bf16[8,24,768]{2,1,0:T(8,128)(2,1)S(1)} collective-permute-done((bf16[8,24,768]{2,1,0:T(8,128)(2,1)S(1)}, bf16[8,24,768]{2,1,0:T(8,128)(2,1)S(1)}, u32[]{:S(2)}, u32[]{:S(2)}) %collective-permute-start.6) | collective-permute-done | bytes 294944 | tf_op jit(solution)/shard_map/ppermute | solution.py:329
  74.9 0.1 add_convert_fusion
  75.0 15.1 %all_to_all.10.terms = bf16[8,24,768]{2,1,0:T(8,128)(2,1)S(1)} all-to-all(bf16[8,24,768]{2,1,0:T(8,128)(2,1)S(1)} %add_convert_fusion), channel_id=1, replica_groups={{0,2,4,6,8,10,12,14},{1,3,5,7,9,11,13,15},{16,18,20,22,24,26,28,30},{17..., dimensions={0} | all-to-all | bytes 589824 | tf_op jit(solution)/shard_map/all_to_all | solution.py:331
  90.0 0.9 finish.1
  (2 shorter events, 0.0 us)
Async XLA Ops:
  0.0 10.9 %copy-start = (f32[9,9,9,9]{3,2,1,0:T(8,128)S(1)}, f32[9,9,9,9]{3,2,1,0:T(8,128)}, u32[]{:S(2)}) copy-start(f32[9,9,9,9]{3,2,1,0:T(8,128)} %param.10) | copy-start | bytes 78736
  3.0 7.8 %copy-start.2 = (s32[9]{0:T(128)S(1)}, s32[9]{0:T(128)}, u32[]{:S(2)}) copy-start(s32[9]{0:T(128)} %constant.4.clone) | copy-start | bytes 112
  3.0 35.1 %all-to-all-start = ((bf16[8,2,144,128]{3,2,1,0:T(8,128)(2,1)}), bf16[8,2,144,128]{3,2,1,0:T(8,128)(2,1)S(1)}, u32[]{:S(2)}, u32[]{:S(2)}) async-start(bf16[8,2,144,128]{3,2,1,0:T(8,128)(2,1)} %get-tuple-element.15), calls=%async_computation | async-start | bytes 1179648 | tf_op jit(solution)/shard_map/all_to_all | solution.py:319
  11.2 0.8 copy-start.1
  38.2 10.6 %collective-permute-start = (bf16[8,144,128]{2,1,0:T(8,128)(2,1)S(1)}, bf16[8,144,128]{2,1,0:T(8,128)(2,1)S(1)}, u32[]{:S(2)}, u32[]{:S(2)}) collective-permute-start(bf16[8,144,128]{2,1,0:T(8,128)(2,1)S(1)} %get-tuple-element.24.own), channel_id=1, source_target_pairs={{0,48},{16,0},{32,16},{48,32},{64,112},{80,64},{96,80},{112,96},{1... | collective-permute-start | bytes 884744 | tf_op jit(solution)/shard_map/ppermute | solution.py:306
  42.5 13.5 %collective-permute-start.4 = (bf16[8,144,128]{2,1,0:T(8,128)(2,1)S(1)}, bf16[8,144,128]{2,1,0:T(8,128)(2,1)S(1)}, u32[]{:S(2)}, u32[]{:S(2)}) collective-permute-start(bf16[8,144,128]{2,1,0:T(8,128)(2,1)S(1)} %get-tuple-element.23.own), channel_id=1, source_target_pairs={{0,16},{16,32},{32,48},{48,0},{64,80},{80,96},{96,112},{112,64},{1... | collective-permute-start | bytes 884744 | tf_op jit(solution)/shard_map/ppermute | solution.py:306
  44.5 15.6 %collective-permute-start.2 = (bf16[8,144,128]{2,1,0:T(8,128)(2,1)S(1)}, bf16[8,144,128]{2,1,0:T(8,128)(2,1)S(1)}, u32[]{:S(2)}, u32[]{:S(2)}) collective-permute-start(bf16[8,144,128]{2,1,0:T(8,128)(2,1)S(1)} %get-tuple-element.24.own), channel_id=1, source_target_pairs={{0,16},{16,32},{32,48},{48,0},{64,80},{80,96},{96,112},{112,64},{1... | collective-permute-start | bytes 884744 | tf_op jit(solution)/shard_map/ppermute | solution.py:306
  48.8 11.3 %collective-permute-start.1 = (bf16[8,144,128]{2,1,0:T(8,128)(2,1)S(1)}, bf16[8,144,128]{2,1,0:T(8,128)(2,1)S(1)}, u32[]{:S(2)}, u32[]{:S(2)}) collective-permute-start(bf16[8,144,128]{2,1,0:T(8,128)(2,1)S(1)} %collective-permute-done.right), channel_id=1, source_target_pairs={{0,48},{16,0},{32,16},{48,32},{64,112},{80,64},{96,80},{112,96},{1... | collective-permute-start | bytes 884744 | tf_op jit(solution)/shard_map/ppermute | solution.py:306
  54.1 11.6 %collective-permute-start.3 = (bf16[8,144,128]{2,1,0:T(8,128)(2,1)S(1)}, bf16[8,144,128]{2,1,0:T(8,128)(2,1)S(1)}, u32[]{:S(2)}, u32[]{:S(2)}) collective-permute-start(bf16[8,144,128]{2,1,0:T(8,128)(2,1)S(1)} %get-tuple-element.23.own), channel_id=1, source_target_pairs={{0,48},{16,0},{32,16},{48,32},{64,112},{80,64},{96,80},{112,96},{1... | collective-permute-start | bytes 884744 | tf_op jit(solution)/shard_map/ppermute | solution.py:306
  56.0 10.4 %collective-permute-start.5 = (bf16[8,144,128]{2,1,0:T(8,128)(2,1)S(1)}, bf16[8,144,128]{2,1,0:T(8,128)(2,1)S(1)}, u32[]{:S(2)}, u32[]{:S(2)}) collective-permute-start(bf16[8,144,128]{2,1,0:T(8,128)(2,1)S(1)} %collective-permute-done.4.left), channel_id=1, source_target_pairs={{0,16},{16,32},{32,48},{48,0},{64,80},{80,96},{96,112},{112,64},{1... | collective-permute-start | bytes 884744 | tf_op jit(solution)/shard_map/ppermute | solution.py:306
  69.6 5.3 %collective-permute-start.6 = (bf16[8,24,768]{2,1,0:T(8,128)(2,1)S(1)}, bf16[8,24,768]{2,1,0:T(8,128)(2,1)S(1)}, u32[]{:S(2)}, u32[]{:S(2)}) collective-permute-start(bf16[8,24,768]{2,1,0:T(8,128)(2,1)S(1)} %get-tuple-element.22), channel_id=1, source_target_pairs={{0,1},{1,0},{2,3},{3,2},{4,5},{5,4},{6,7},{7,6},{8,9},{9,8},{10,11... | collective-permute-start | bytes 884744 | tf_op jit(solution)/shard_map/ppermute | solution.py:329

commit v4 on v3

--- a/solution.py
+++ b/solution.py
@@ -1,3 +1,5 @@
+import functools
+
 import jax
 import jax.numpy as jnp
 from jax import lax
@@ -100,22 +102,22 @@
     dense = nn(one_hot((b == (a // XB) * 16 + a % XB) & (a < 108)), up_s[0].astype(BF)).astype(BF)
     a, b = iota((192, 192), 0), iota((192, 192), 1)
     edge = nt(one_hot(b == (a % JB) * SEC + a // JB), dense).astype(BF)
-    a, b = iota((96, 144), 0), iota((96, 144), 1)
-    lower_16 = up_s[1].astype(BF)
-    sector = iota((96, 192), 0) // XB
-    column = iota((96, 192), 1) % SEC
+    a, b = iota((DD * 96, 144), 0), iota((DD * 96, 144), 1)
+    pos = a // 96
+    l = jnp.where(pos == 4, ORDER[4], jnp.where(pos == 5, ORDER[5], pos))
+    copies = nn(one_hot(b == l * 16 + a % XB), up_s[1].astype(BF))
+    sector = iota((96, 192), 0) // XB - iota((96, 192), 1) % SEC
     for n, l in enumerate(ORDER):
-        copies = nn(one_hot(b == l * 16 + a % XB), lower_16)
-        wide_s[:, n * 256:n * 256 + 192] = jnp.where(
-            column == sector - CHARGE[l], copies, 0.0
+        wide_s[n * 96:(n + 1) * 96, :] = jnp.where(
+            sector == CHARGE[l], copies[n * 96:(n + 1) * 96], 0.0
         ).astype(BF)
-        wide_s[:, n * 256 + 192:(n + 1) * 256] = jnp.zeros((96, 64), BF)
-    a, b = iota((DD * 256, 256), 0), iota((DD * 256, 256), 1)
-    fold = one_hot(b == (a // 256) * JB + (a % 256) // SEC)
-    grid = nn(wide_s[...], fold)
-    pack[1] = grid[:, 0:192]
+    a, b = iota((192, 128), 0), iota((192, 128), 1)
+    folded = nn(wide_s[...], one_hot(b == a // SEC))
+    for n in range(SEC):
+        pack[1, :, n * JB:(n + 1) * JB] = folded[n * 96:(n + 1) * 96, 0:JB]
     for v, (host, at) in enumerate(OUT_PLACES):
-        pack[1, host * XB:(host + 1) * XB, at * JB:(at + 1) * JB] = grid[v * XB:(v + 1) * XB, 192:216]
+        row = SEC * 96 + v * XB
+        pack[1, host * XB:(host + 1) * XB, at * JB:(at + 1) * JB] = folded[row:row + XB, 0:JB]
     for n in range(NY):
         for side in range(2):
             lb_out[n, side, 0:96, :] = pack[side, :, 0:128].astype(BF)
@@ -136,7 +138,7 @@
         scratch_shapes=[
             pltpu.VMEM((216, 96), F32),
             pltpu.VMEM((2, 144, 192), F32),
-            pltpu.VMEM((96, DD * 256), BF),
+            pltpu.VMEM((DD * 96, 192), BF),
             pltpu.VMEM((2, 96, 192), F32),
         ],
         compiler_params=WIDE,
@@ -144,10 +146,15 @@
     )(sizes, left, upper, lower)
 
 
-def regrouping(turn):
-    a, b = iota((384, 384), 0), iota((384, 384), 1)
-    d = ((a % 48) // XB + turn + NX - lax.axis_index("up") % NX) % NX
-    return one_hot(b == d * 96 + (a // 48) * XB + a % XB)
+def charge_of(member):
+    return member // 3 - member % 3
+
+
+def regrouping(turn, count):
+    a, b = iota((count * 96, 384), 0), iota((count * 96, 384), 1)
+    size = count * XB
+    d = ((a % size) // XB + turn + NX - lax.axis_index("up") % NX) % NX
+    return one_hot(b == d * 96 + (a // size) * XB + a % XB)
 
 
 def regrouped(regroup, pieces, g):
@@ -161,16 +168,17 @@
 
 def spread_out(part, charge, hosts, sector):
     lane = iota((1, 192), 1) // JB
-    rows = part[sector * 48:(sector + 1) * 48]
+    size = part.shape[0] // SEC
+    rows = part[sector * size:(sector + 1) * size]
     for n in range(SEC):
         if not 0 <= sector + charge[ORDER[n]] < SEC:
             rows = jnp.where(lane == n, jnp.zeros((), BF), rows)
     host, spot = hosts[sector]
-    return rows, part[host * 48:(host + 1) * 48, spot * JB:(spot + 1) * JB]
-
-
-def mix_kernel(site, u, own, right, far, left, mixed, left_q, moved, at, wide):
-    regroup = regrouping(0)
+    return rows, part[host * size:(host + 1) * size, spot * JB:(spot + 1) * JB]
+
+
+def mix_kernel(site, u, own, right, far, left, spread, left_q, image, moved, merged, mixed):
+    regroup = regrouping(0, NX)
     left_q[...] = jnp.zeros(left_q.shape, BF)
     moved[...] = jnp.zeros(moved.shape, F32)
     for g in range(NY):
@@ -181,58 +189,46 @@
             left_q[q, g * 48:(g + 1) * 48, 192:216] = last
     for q in range(SEC):
         columns = u[:, q * JB:(q + 1) * JB, :].reshape(CAP, 128)
-        image = tn(columns, left_q[q])
+        image[q * 128:(q + 1) * 128, :] = tn(columns, left_q[q]).astype(BF)
+    a, b = iota((256, 384), 0), iota((256, 384), 1)
+    inside = b % 128
+    order = one_hot((a == (inside // 8) * JB + (b // 128) * 8 + inside % 8) & (inside < 72))
+    parted = nn(image[...], order)
+    for q in range(SEC):
         for k in range(DD):
             p = q + CHARGE[k]
             if 0 <= p < SEC:
-                moved[p * XB:(p + 1) * XB, k * 256:(k + 1) * 256] = image[k * XB:(k + 1) * XB]
-    at[...] = moved[...].astype(BF)
-    a, b = iota((81, DD * 256), 0), iota((81, DD * 256), 1)
-    pos = (b % 256) // JB
+                rows = parted[q * 128 + k * XB:q * 128 + (k + 1) * XB]
+                for part in range(3):
+                    moved[part * 128 + p * XB:part * 128 + (p + 1) * XB, k * 128:(k + 1) * 128] = (
+                        rows[:, part * 128:(part + 1) * 128]
+                    )
+    a, b = iota((81, DD * 128), 0), iota((81, DD * 128), 1)
+    pos = (b % 128) // 8
     s = jnp.where(pos == 4, ORDER[4], jnp.where(pos == 5, ORDER[5], pos))
-    widen = one_hot((s + (b // 256) * DD == a) & (pos < DD))
-    wide[...] = nn(site[...].astype(BF), widen)
-    a, b = iota((JB, DD * 256), 0), iota((JB, DD * 256), 1)
-    same = ((b % 256) % JB == a) & (b % 256 < 216)
+    a, b = iota((81, 81), 0), iota((81, 81), 1)
+    even = charge_of(b // DD) + charge_of(a // DD) == charge_of(b % DD) + charge_of(a % DD)
+    allowed = jnp.where(even, site[...], 0.0).astype(BF)
+    a, b = iota((81, DD * 128), 0), iota((81, DD * 128), 1)
+    wide = nn(allowed, one_hot((s + (b // 128) * DD == a) & (pos < DD)))
+    a, b = iota((8, DD * 128), 0), iota((8, DD * 128), 1)
+    same = (b % 8 == a) & (b % 128 < 72)
+    weights = [
+        jnp.where(same, wide[r * DD + l:r * DD + l + 1, :], 0.0) for r in ORDER for l in ORDER
+    ]
+    weights = jnp.concatenate(weights, axis=0).astype(BF)
+    product = nt(weights, moved[...].astype(BF))
+    for n in range(DD):
+        for part in range(3):
+            block = product[n * 72:(n + 1) * 72, part * 128:part * 128 + 96].reshape(DD, 8, 96)
+            if n < SEC:
+                merged[:, part, :, n * 96:(n + 1) * 96] = block
+                continue
+            for p, (host, spot) in enumerate(IN_PLACES):
+                start = spot * 96 + host * XB
+                merged[:, part, :, start:start + XB] = block[:, :, p * XB:(p + 1) * XB]
+    mixed[0:216, :] = merged[...].reshape(216, SEC * 96).astype(BF)
     mixed[216:256, :] = jnp.zeros((40, SEC * 96), BF)
-    last = None
-    for n, r in enumerate(ORDER):
-        rows = [jnp.where(same, wide[r * DD + l:r * DD + l + 1, :], 0.0).astype(BF) for l in ORDER]
-        last = nt(jnp.concatenate(rows, axis=0), at[...]).astype(BF)
-        if n < SEC:
-            mixed[0:216, n * 96:(n + 1) * 96] = last
-    for p, (host, spot) in enumerate(IN_PLACES):
-        start = spot * 96 + host * XB
-        mixed[0:216, start:start + XB] = last[:, p * XB:(p + 1) * XB]
-
-
-def mix(site, u, pieces):
-    return pl.pallas_call(
-        mix_kernel,
-        out_shape=jax.ShapeDtypeStruct((256, SEC * 96), BF),
-        in_specs=[VMEM] * 6,
-        out_specs=VMEM,
-        scratch_shapes=[
-            pltpu.VMEM((SEC, CAP, 256), BF),
-            pltpu.VMEM((96, DD * 256), F32),
-            pltpu.VMEM((96, DD * 256), BF),
-            pltpu.VMEM((81, DD * 256), F32),
-        ],
-        compiler_params=PARAMS,
-        cost_estimate=pl.CostEstimate(flops=6_000_000_000, bytes_accessed=3_000_000, transcendentals=0),
-        name="mix",
-    )(site, u, *pieces)
-
-
-def lower_kernel(mixed, own, right, far, left, ours, theirs, lower_v, spread):
-    regroup = regrouping(2 * lax.rem(lax.axis_index("lo"), 2))
-    lower_v[...] = jnp.zeros(lower_v.shape, BF)
-    for g in range(NY):
-        part = regrouped(regroup, (own, right, far, left), g)
-        for v in range(SEC):
-            rows, last = spread_out(part, [-c for c in CHARGE], OUT_PLACES, v)
-            lower_v[g * 48:(g + 1) * 48, v * 256:v * 256 + 192] = rows
-            lower_v[g * 48:(g + 1) * 48, v * 256 + 192:v * 256 + 216] = last
     lane = iota((1, SEC * 96), 1)
     sector = (lane % 96) // XB
     for n in range(SEC):
@@ -241,30 +237,53 @@
         sector = jnp.where(lane // XB == spot * SEC + host, p, sector)
     for v in range(SEC):
         spread[v * 256:(v + 1) * 256, :] = jnp.where(sector == v, mixed[...], jnp.zeros((), BF))
+
+
+def mix(site, u, pieces):
+    return pl.pallas_call(
+        mix_kernel,
+        out_shape=jax.ShapeDtypeStruct((SEC * 256, SEC * 96), BF),
+        in_specs=[VMEM] * 6,
+        out_specs=VMEM,
+        scratch_shapes=[
+            pltpu.VMEM((SEC, CAP, 256), BF),
+            pltpu.VMEM((SEC * 128, 256), BF),
+            pltpu.VMEM((3 * 128, DD * 128), F32),
+            pltpu.VMEM((DD, 3, 8, SEC * 96), F32),
+            pltpu.VMEM((256, SEC * 96), BF),
+        ],
+        compiler_params=PARAMS,
+        cost_estimate=pl.CostEstimate(flops=6_000_000_000, bytes_accessed=3_000_000, transcendentals=0),
+        name="mix",
+    )(site, u, *pieces)
+
+
+def lower_kernel(half, spread, own, right, far, left, out, lower_v):
+    regroup = regrouping(2 * lax.rem(lax.axis_index("lo") + half, 2), 2)
+    lower_v[...] = jnp.zeros(lower_v.shape, BF)
+    for g in range(NY):
+        part = regrouped(regroup, (own, right, far, left), g)
+        for v in range(SEC):
+            rows, last = spread_out(part, [-c for c in CHARGE], OUT_PLACES, v)
+            lower_v[g * JB:(g + 1) * JB, v * 256:v * 256 + 192] = rows
+            lower_v[g * JB:(g + 1) * JB, v * 256 + 192:v * 256 + 216] = last
     for n in range(3):
         cut = slice(n * 256, (n + 1) * 256)
         total = nn(lower_v[...], spread[:, cut])
-        for g in range(NY):
-            ours[g, :, cut] = total[g * 48:g * 48 + 24]
-            theirs[g, :, cut] = total[g * 48 + 24:(g + 1) * 48].astype(BF)
-
-
-def contract_lower(mixed, pieces):
+        out[:, :, cut] = total.reshape(NY, JB, 256).astype(out.dtype)
+
+
+def contract_lower(half, spread, pieces):
     return pl.pallas_call(
-        lower_kernel,
-        out_shape=(
-            jax.ShapeDtypeStruct((NY, JB, SEC * 96), F32),
-            jax.ShapeDtypeStruct((NY, JB, SEC * 96), BF),
-        ),
+        functools.partial(lower_kernel, half),
+        out_shape=jax.ShapeDtypeStruct((NY, JB, SEC * 96), BF if half else F32),
         in_specs=[VMEM] * 5,
-        out_specs=(VMEM, VMEM),
-        scratch_shapes=[
-            pltpu.VMEM((CAP, SEC * 256), BF),
-            pltpu.VMEM((SEC * 256, SEC * 96), BF),
-        ],
+        out_specs=VMEM,
+        scratch_shapes=[pltpu.VMEM((NY * JB, SEC * 256), BF)],
         compiler_params=PARAMS,
-        name="lower",
-    )(mixed, *pieces)
+        cost_estimate=pl.CostEstimate(flops=3_000_000_000, bytes_accessed=3_000_000, transcendentals=0),
+        name="lower_theirs" if half else "lower_ours",
+    )(spread, *pieces)
 
 
 def finish_kernel(terms, out, stacked):
@@ -307,24 +326,19 @@
 
 
 def local(sector_sizes, left, upper_edge, lower_edge, site_block):
-    charges = jnp.array(CHARGE, dtype=jnp.int32)
     lb, u = prepare(sector_sizes, left, upper_edge, lower_edge)
-    site_block, lb = lax.optimization_barrier((site_block, lb))
-    even = (
-        charges[:, None, None, None] + charges[None, None, :, None]
-        == charges[None, :, None, None] + charges[None, None, None, :]
-    )
-    site = jnp.where(even, site_block, jnp.float32(0.0))
-    site = site.transpose(2, 3, 0, 1).reshape(81, 81)
     line = lax.all_to_all(lb, "up", 0, 0, axis_index_groups=Y_GROUPS)
     u = lax.all_gather(u, "lo", axis=0)
-    line, u, site = lax.optimization_barrier((line, u, site))
+    line, u, site_block = lax.optimization_barrier((line, u, site_block))
+    site = site_block.transpose(2, 3, 0, 1).reshape(81, 81)
     left, lower = line[:, 0], line[:, 1]
     left_right, left_left = from_x(left, 1), from_x(left, -1)
     lower_right, lower_left = from_x(lower, 1), from_x(lower, -1)
     left_far, lower_far = from_x(left_right, 1), from_x(lower_left, -1)
-    mixed = mix(site, u, (left, left_right, left_far, left_left))
-    ours, theirs = contract_lower(mixed, (lower, lower_right, lower_far, lower_left))
+    spread = mix(site, u, (left, left_right, left_far, left_left))
+    lines = (lower, lower_right, lower_far, lower_left)
+    theirs = contract_lower(1, spread, lines)
+    ours = contract_lower(0, spread, lines)
     swap = [(n, n + 1 - 2 * (n % 2)) for n in range(N_LO)]
     theirs = lax.ppermute(theirs, "lo", swap)
     terms = (ours + theirs.astype(F32)).astype(BF)

time: 91.7 us -> 91.2 us (level)
  Pallas kernels: 12.5 us -> 11 us
    ppermute x6, waiting for transfers between devices: 3.87 us -> 5.47 us  [from_x(): return lax.ppermute(value, 'up', pairs)]
    reshape x2, local copies, waits for them, and re-layouts: 0.3 us -> 1.7 us  [local(): site = site_block.transpose(2, 3, 0, 1).reshape(81, 81)]
    pallas_call x2 -> x3, Pallas kernels: 8.55 us -> 7.3 us  [the longest x1 3.7 us: mix(): pl.pallas_call(mix_kernel, out_shape=jax.ShapeDtypeStruct((SEC * 256, SEC...]
    ppermute x1, waiting for transfers between devices: 1.19 us -> 0.01 us  [local(): theirs = lax.ppermute(theirs, 'lo', swap)]
  transfers between devices with their start and end apart: 8 -> 8, of which waited for: 5 -> 3; matrix products, arithmetic and copies ran while one was open for 1% -> 2% of each run, Pallas kernels for 6% -> 6%
where the time goes in v4:
time: 91.2 us; the launch traced here: 90.7 us
  blocking collectives  41.5 us (46%)
  starting transfers between devices  30.7 us (34%)
  Pallas kernels  11 us (12%)
  waiting for transfers between devices  5.48 us (6%)
  local copies, waits for them, and re-layouts  1.74 us (2%)
    all_gather x1, blocking collectives, local(): u = lax.all_gather(u, 'lo', axis=0)  26.3 us
    ppermute x6, starting transfers between devices, from_x(): return lax.ppermute(value, 'up', pairs)  19 us
    all_to_all x1, blocking collectives, local(): terms = lax.all_to_all(terms, 'lo', 0, 0, axis_index_groups=Z_GROUPS)  15.2 us
    all_to_all x1, starting transfers between devices, local(): line = lax.all_to_all(lb, 'up', 0, 0, axis_index_groups=Y_GROUPS)  7.65 us
    ppermute x6, waiting for transfers between devices, from_x(): return lax.ppermute(value, 'up', pairs)  5.47 us
    ppermute x1, starting transfers between devices, local(): theirs = lax.ppermute(theirs, 'lo', swap)  4.07 us
    pallas_call x1, Pallas kernels, mix(): pl.pallas_call(mix_kernel, out_shape=jax.ShapeDtypeStruct((SEC * 256, SEC...  3.7 us
    pallas_call x2, Pallas kernels, contract_lower(): pl.pallas_call(functools.partial(lower_kernel, half), out_shape=jax.Shape...  3.6 us
  transfers between devices with their start and end apart: 8, of which 3 were waited for; matrix products, arithmetic and copies ran while one was open for 2% of the time, Pallas kernels for 6%

profile of v4, /device:TPU:1, one launch (start us, length us, event | category | flops | bytes accessed | tf_op | source)
XLA Modules:
  0.0 90.7 jit_solution(5656923557917829676)
XLA Ops:
  0.0 0.0 copy-start
  0.0 2.9 %prepare.1 = (bf16[8,2,144,128]{3,2,1,0:T(8,128)(2,1)}, bf16[192,128]{1,0:T(8,128)(2,1)}) custom-call(s32[8]{0:T(128)} %sizes.1, bf16[9,24,96]{2,1,0:T(8,128)(2,1)} %left.1, bf16[9,12,192]{2,1,0:T(8,128)(2,1)} %upper.1, bf16[9,12,192]{2,1,0:T(8,128)(2,1)} %lower.1), custom_call_target="tpu_custom_call" | custom-call | tf_op jit(solution)/shard_map/prepare/pallas_call | solution.py:130
  2.9 7.7 %all-to-all-start = ((bf16[8,2,144,128]{3,2,1,0:T(8,128)(2,1)}), bf16[8,2,144,128]{3,2,1,0:T(8,128)(2,1)S(1)}, u32[]{:S(2)}, u32[]{:S(2)}) async-start(bf16[8,2,144,128]{3,2,1,0:T(8,128)(2,1)} %get-tuple-element.10), calls=%async_computation | async-start | bytes 1179648 | tf_op jit(solution)/shard_map/all_to_all | solution.py:330
  10.5 26.3 %all-gather = bf16[3072,128]{1,0:T(8,128)(2,1)S(1)} all-gather(bf16[192,128]{1,0:T(8,128)(2,1)} %get-tuple-element.11), channel_id=2, replica_groups=mesh['up'=32,'lo'=16] {'lo'}, dimensions={0}, use_global_device_ids=true | all-gather | bytes 835584 | tf_op jit(solution)/shard_map/all_gather | solution.py:331
  36.9 0.0 all-to-all-done
  36.9 4.4 %collective-permute-start = (bf16[8,144,128]{2,1,0:T(8,128)(2,1)S(1)}, bf16[8,144,128]{2,1,0:T(8,128)(2,1)S(1)}, u32[]{:S(2)}, u32[]{:S(2)}) collective-permute-start(bf16[8,144,128]{2,1,0:T(8,128)(2,1)S(1)} %get-tuple-element.16.own), channel_id=1, source_target_pairs={{0,48},{16,0},{32,16},{48,32},{64,112},{80,64},{96,80},{112,96},{1... | collective-permute-start | bytes 884744 | tf_op jit(solution)/shard_map/ppermute | solution.py:325
  41.3 1.9 %collective-permute-start.4 = (bf16[8,144,128]{2,1,0:T(8,128)(2,1)S(1)}, bf16[8,144,128]{2,1,0:T(8,128)(2,1)S(1)}, u32[]{:S(2)}, u32[]{:S(2)}) collective-permute-start(bf16[8,144,128]{2,1,0:T(8,128)(2,1)S(1)} %get-tuple-element.15.own), channel_id=1, source_target_pairs={{0,16},{16,32},{32,48},{48,0},{64,80},{80,96},{96,112},{112,64},{1... | collective-permute-start | bytes 884744 | tf_op jit(solution)/shard_map/ppermute | solution.py:325
  43.2 2.1 %collective-permute-start.2 = (bf16[8,144,128]{2,1,0:T(8,128)(2,1)S(1)}, bf16[8,144,128]{2,1,0:T(8,128)(2,1)S(1)}, u32[]{:S(2)}, u32[]{:S(2)}) collective-permute-start(bf16[8,144,128]{2,1,0:T(8,128)(2,1)S(1)} %get-tuple-element.16.own), channel_id=1, source_target_pairs={{0,16},{16,32},{32,48},{48,0},{64,80},{80,96},{96,112},{112,64},{1... | collective-permute-start | bytes 884744 | tf_op jit(solution)/shard_map/ppermute | solution.py:325
  45.3 2.2 %collective-permute-done.right = bf16[8,144,128]{2,1,0:T(8,128)(2,1)S(1)} collective-permute-done((bf16[8,144,128]{2,1,0:T(8,128)(2,1)S(1)}, bf16[8,144,128]{2,1,0:T(8,128)(2,1)S(1)}, u32[]{:S(2)}, u32[]{:S(2)}) %collective-permute-start) | collective-permute-done | bytes 294944 | tf_op jit(solution)/shard_map/ppermute | solution.py:325
  47.5 5.3 %collective-permute-start.1 = (bf16[8,144,128]{2,1,0:T(8,128)(2,1)S(1)}, bf16[8,144,128]{2,1,0:T(8,128)(2,1)S(1)}, u32[]{:S(2)}, u32[]{:S(2)}) collective-permute-start(bf16[8,144,128]{2,1,0:T(8,128)(2,1)S(1)} %collective-permute-done.right), channel_id=1, source_target_pairs={{0,48},{16,0},{32,16},{48,32},{64,112},{80,64},{96,80},{112,96},{1... | collective-permute-start | bytes 884744 | tf_op jit(solution)/shard_map/ppermute | solution.py:325
  52.8 1.9 %collective-permute-start.3 = (bf16[8,144,128]{2,1,0:T(8,128)(2,1)S(1)}, bf16[8,144,128]{2,1,0:T(8,128)(2,1)S(1)}, u32[]{:S(2)}, u32[]{:S(2)}) collective-permute-start(bf16[8,144,128]{2,1,0:T(8,128)(2,1)S(1)} %get-tuple-element.15.own), channel_id=1, source_target_pairs={{0,48},{16,0},{32,16},{48,32},{64,112},{80,64},{96,80},{112,96},{1... | collective-permute-start | bytes 884744 | tf_op jit(solution)/shard_map/ppermute | solution.py:325
  54.8 0.0 copy-done
  54.8 0.8 reshape.5
  55.6 0.9 copy.11.site
  56.5 0.0 collective-permute-done.4.left
  56.5 3.4 %collective-permute-start.5 = (bf16[8,144,128]{2,1,0:T(8,128)(2,1)S(1)}, bf16[8,144,128]{2,1,0:T(8,128)(2,1)S(1)}, u32[]{:S(2)}, u32[]{:S(2)}) collective-permute-start(bf16[8,144,128]{2,1,0:T(8,128)(2,1)S(1)} %collective-permute-done.4.left), channel_id=1, source_target_pairs={{0,16},{16,32},{32,48},{48,0},{64,80},{80,96},{96,112},{112,64},{1... | collective-permute-start | bytes 884744 | tf_op jit(solution)/shard_map/ppermute | solution.py:325
  59.9 0.0 collective-permute-done.2.left
  59.9 0.0 collective-permute-done.1.far
  59.9 3.7 %mix.1.spread = bf16[2048,768]{1,0:T(8,128)(2,1)S(1)} custom-call(f32[81,81]{1,0:T(8,128)S(1)} %copy.11.site, bf16[16,192,128]{2,1,0:T(8,128)(2,1)S(1)} %bitcast.8, bf16[8,144,128]{2,1,0:T(8,128)(2,1)S(1)} %get-tuple-element.16.own, bf16[8,144,128]{2,1,0:T(8,128)(2,1)S(1)} %collective-permute-done.right, ...), custom_call_target="tpu_custom_call" | custom-call | flops 6000000000 | bytes 3000000 | tf_op jit(solution)/shard_map/mix/pallas_call | solution.py:243
  63.6 0.9 collective-permute-done.3.right
  64.5 2.4 %collective-permute-done.5.far = bf16[8,144,128]{2,1,0:T(8,128)(2,1)S(1)} collective-permute-done((bf16[8,144,128]{2,1,0:T(8,128)(2,1)S(1)}, bf16[8,144,128]{2,1,0:T(8,128)(2,1)S(1)}, u32[]{:S(2)}, u32[]{:S(2)}) %collective-permute-start.5) | collective-permute-done | bytes 294944 | tf_op jit(solution)/shard_map/ppermute | solution.py:325
  66.9 1.8 %lower_theirs.1 = bf16[8,24,768]{2,1,0:T(8,128)(2,1)S(1)} custom-call(bf16[2048,768]{1,0:T(8,128)(2,1)S(1)} %mix.1.spread, bf16[8,144,128]{2,1,0:T(8,128)(2,1)S(1)} %get-tuple-element.15.own, bf16[8,144,128]{2,1,0:T(8,128)(2,1)S(1)} %collective-permute-done.3.right, bf16[8,144,128]{2,1,0:T(8,128)(2,1)S(1)} %collective-permute-done.5.far, ...), custom_call_target="tpu_custom_call" | custom-call | flops 3000000000 | bytes 3000000 | tf_op jit(solution)/shard_map/lower_theirs/pallas_call | solution.py:277
  68.7 4.1 %collective-permute-start.6 = (bf16[8,24,768]{2,1,0:T(8,128)(2,1)S(1)}, bf16[8,24,768]{2,1,0:T(8,128)(2,1)S(1)}, u32[]{:S(2)}, u32[]{:S(2)}) collective-permute-start(bf16[8,24,768]{2,1,0:T(8,128)(2,1)S(1)} %lower_theirs.1), channel_id=1, source_target_pairs={{0,1},{1,0},{2,3},{3,2},{4,5},{5,4},{6,7},{7,6},{8,9},{9,8},{10,11... | collective-permute-start | bytes 884744 | tf_op jit(solution)/shard_map/ppermute | solution.py:343
  72.7 1.8 %lower_ours.1 = f32[8,24,768]{2,1,0:T(8,128)S(1)} custom-call(bf16[2048,768]{1,0:T(8,128)(2,1)S(1)} %mix.1.spread, bf16[8,144,128]{2,1,0:T(8,128)(2,1)S(1)} %get-tuple-element.15.own, bf16[8,144,128]{2,1,0:T(8,128)(2,1)S(1)} %collective-permute-done.3.right, bf16[8,144,128]{2,1,0:T(8,128)(2,1)S(1)} %collective-permute-done.5.far, ...), custom_call_target="tpu_custom_call" | custom-call | flops 3000000000 | bytes 3000000 | tf_op jit(solution)/shard_map/lower_ours/pallas_call | solution.py:277
  74.5 0.0 collective-permute-done.6
  74.6 0.1 add_convert_fusion
  74.6 15.2 %all_to_all.10.terms = bf16[8,24,768]{2,1,0:T(8,128)(2,1)S(1)} all-to-all(bf16[8,24,768]{2,1,0:T(8,128)(2,1)S(1)} %add_convert_fusion), channel_id=1, replica_groups={{0,2,4,6,8,10,12,14},{1,3,5,7,9,11,13,15},{16,18,20,22,24,26,28,30},{17..., dimensions={0} | all-to-all | bytes 589824 | tf_op jit(solution)/shard_map/all_to_all | solution.py:345
  89.8 0.9 finish.1
  (1 shorter events, 0.0 us)
Async XLA Ops:
  0.0 54.8 %copy-start = (f32[9,9,9,9]{3,2,1,0:T(8,128)S(1)}, f32[9,9,9,9]{3,2,1,0:T(8,128)}, u32[]{:S(2)}) copy-start(f32[9,9,9,9]{3,2,1,0:T(8,128)} %param.9) | copy-start | bytes 78736
  2.9 34.0 %all-to-all-start = ((bf16[8,2,144,128]{3,2,1,0:T(8,128)(2,1)}), bf16[8,2,144,128]{3,2,1,0:T(8,128)(2,1)S(1)}, u32[]{:S(2)}, u32[]{:S(2)}) async-start(bf16[8,2,144,128]{3,2,1,0:T(8,128)(2,1)} %get-tuple-element.10), calls=%async_computation | async-start | bytes 1179648 | tf_op jit(solution)/shard_map/all_to_all | solution.py:330
  36.9 10.6 %collective-permute-start = (bf16[8,144,128]{2,1,0:T(8,128)(2,1)S(1)}, bf16[8,144,128]{2,1,0:T(8,128)(2,1)S(1)}, u32[]{:S(2)}, u32[]{:S(2)}) collective-permute-start(bf16[8,144,128]{2,1,0:T(8,128)(2,1)S(1)} %get-tuple-element.16.own), channel_id=1, source_target_pairs={{0,48},{16,0},{32,16},{48,32},{64,112},{80,64},{96,80},{112,96},{1... | collective-permute-start | bytes 884744 | tf_op jit(solution)/shard_map/ppermute | solution.py:325
  41.3 15.2 %collective-permute-start.4 = (bf16[8,144,128]{2,1,0:T(8,128)(2,1)S(1)}, bf16[8,144,128]{2,1,0:T(8,128)(2,1)S(1)}, u32[]{:S(2)}, u32[]{:S(2)}) collective-permute-start(bf16[8,144,128]{2,1,0:T(8,128)(2,1)S(1)} %get-tuple-element.15.own), channel_id=1, source_target_pairs={{0,16},{16,32},{32,48},{48,0},{64,80},{80,96},{96,112},{112,64},{1... | collective-permute-start | bytes 884744 | tf_op jit(solution)/shard_map/ppermute | solution.py:325
  43.2 16.6 %collective-permute-start.2 = (bf16[8,144,128]{2,1,0:T(8,128)(2,1)S(1)}, bf16[8,144,128]{2,1,0:T(8,128)(2,1)S(1)}, u32[]{:S(2)}, u32[]{:S(2)}) collective-permute-start(bf16[8,144,128]{2,1,0:T(8,128)(2,1)S(1)} %get-tuple-element.16.own), channel_id=1, source_target_pairs={{0,16},{16,32},{32,48},{48,0},{64,80},{80,96},{96,112},{112,64},{1... | collective-permute-start | bytes 884744 | tf_op jit(solution)/shard_map/ppermute | solution.py:325
  47.5 12.3 %collective-permute-start.1 = (bf16[8,144,128]{2,1,0:T(8,128)(2,1)S(1)}, bf16[8,144,128]{2,1,0:T(8,128)(2,1)S(1)}, u32[]{:S(2)}, u32[]{:S(2)}) collective-permute-start(bf16[8,144,128]{2,1,0:T(8,128)(2,1)S(1)} %collective-permute-done.right), channel_id=1, source_target_pairs={{0,48},{16,0},{32,16},{48,32},{64,112},{80,64},{96,80},{112,96},{1... | collective-permute-start | bytes 884744 | tf_op jit(solution)/shard_map/ppermute | solution.py:325
  52.8 11.6 %collective-permute-start.3 = (bf16[8,144,128]{2,1,0:T(8,128)(2,1)S(1)}, bf16[8,144,128]{2,1,0:T(8,128)(2,1)S(1)}, u32[]{:S(2)}, u32[]{:S(2)}) collective-permute-start(bf16[8,144,128]{2,1,0:T(8,128)(2,1)S(1)} %get-tuple-element.15.own), channel_id=1, source_target_pairs={{0,48},{16,0},{32,16},{48,32},{64,112},{80,64},{96,80},{112,96},{1... | collective-permute-start | bytes 884744 | tf_op jit(solution)/shard_map/ppermute | solution.py:325
  56.5 10.4 %collective-permute-start.5 = (bf16[8,144,128]{2,1,0:T(8,128)(2,1)S(1)}, bf16[8,144,128]{2,1,0:T(8,128)(2,1)S(1)}, u32[]{:S(2)}, u32[]{:S(2)}) collective-permute-start(bf16[8,144,128]{2,1,0:T(8,128)(2,1)S(1)} %collective-permute-done.4.left), channel_id=1, source_target_pairs={{0,16},{16,32},{32,48},{48,0},{64,80},{80,96},{96,112},{112,64},{1... | collective-permute-start | bytes 884744 | tf_op jit(solution)/shard_map/ppermute | solution.py:325
  68.7 5.9 %collective-permute-start.6 = (bf16[8,24,768]{2,1,0:T(8,128)(2,1)S(1)}, bf16[8,24,768]{2,1,0:T(8,128)(2,1)S(1)}, u32[]{:S(2)}, u32[]{:S(2)}) collective-permute-start(bf16[8,24,768]{2,1,0:T(8,128)(2,1)S(1)} %lower_theirs.1), channel_id=1, source_target_pairs={{0,1},{1,0},{2,3},{3,2},{4,5},{5,4},{6,7},{7,6},{8,9},{9,8},{10,11... | collective-permute-start | bytes 884744 | tf_op jit(solution)/shard_map/ppermute | solution.py:343

commit v5 on v4

--- a/solution.py
+++ b/solution.py
@@ -177,7 +177,7 @@
     return rows, part[host * size:(host + 1) * size, spot * JB:(spot + 1) * JB]
 
 
-def mix_kernel(site, u, own, right, far, left, spread, left_q, image, moved, merged, mixed):
+def mix_kernel(site, u, own, right, far, left, spread, left_q, image, moved, merged, mixed, legs):
     regroup = regrouping(0, NX)
     left_q[...] = jnp.zeros(left_q.shape, BF)
     moved[...] = jnp.zeros(moved.shape, F32)
@@ -203,18 +203,24 @@
                     moved[part * 128 + p * XB:part * 128 + (p + 1) * XB, k * 128:(k + 1) * 128] = (
                         rows[:, part * 128:(part + 1) * 128]
                     )
+    for n in range(DD * DD):
+        legs[n * 16:n * 16 + DD, 0:DD] = site[n // DD, n % DD]
     a, b = iota((81, DD * 128), 0), iota((81, DD * 128), 1)
     pos = (b % 128) // 8
     s = jnp.where(pos == 4, ORDER[4], jnp.where(pos == 5, ORDER[5], pos))
-    a, b = iota((81, 81), 0), iota((81, 81), 1)
-    even = charge_of(b // DD) + charge_of(a // DD) == charge_of(b % DD) + charge_of(a % DD)
-    allowed = jnp.where(even, site[...], 0.0).astype(BF)
-    a, b = iota((81, DD * 128), 0), iota((81, DD * 128), 1)
-    wide = nn(allowed, one_hot((s + (b // 128) * DD == a) & (pos < DD)))
+    widen = one_hot((s + (b // 128) * DD == a) & (pos < DD))
+    l, b = iota((16, DD * 128), 0), iota((16, DD * 128), 1)
+    pos = (b % 128) // 8
+    s = jnp.where(pos == 4, ORDER[4], jnp.where(pos == 5, ORDER[5], pos))
+    balance = charge_of(b // 128) - charge_of(s) - charge_of(l)
+    wide = []
+    for r in range(DD):
+        rows = tn(legs[pl.ds(r, DD * DD, stride=16), :].astype(BF), widen)[0:16]
+        wide.append(jnp.where(balance == -CHARGE[r], rows, 0.0))
     a, b = iota((8, DD * 128), 0), iota((8, DD * 128), 1)
     same = (b % 8 == a) & (b % 128 < 72)
     weights = [
-        jnp.where(same, wide[r * DD + l:r * DD + l + 1, :], 0.0) for r in ORDER for l in ORDER
+        jnp.where(same, wide[r][l:l + 1, :], 0.0) for r in ORDER for l in ORDER
     ]
     weights = jnp.concatenate(weights, axis=0).astype(BF)
     product = nt(weights, moved[...].astype(BF))
@@ -251,6 +257,7 @@
             pltpu.VMEM((3 * 128, DD * 128), F32),
             pltpu.VMEM((DD, 3, 8, SEC * 96), F32),
             pltpu.VMEM((256, SEC * 96), BF),
+            pltpu.VMEM((DD * DD * 16, 128), F32),
         ],
         compiler_params=PARAMS,
         cost_estimate=pl.CostEstimate(flops=6_000_000_000, bytes_accessed=3_000_000, transcendentals=0),
@@ -329,13 +336,12 @@
     lb, u = prepare(sector_sizes, left, upper_edge, lower_edge)
     line = lax.all_to_all(lb, "up", 0, 0, axis_index_groups=Y_GROUPS)
     u = lax.all_gather(u, "lo", axis=0)
-    line, u, site_block = lax.optimization_barrier((line, u, site_block))
-    site = site_block.transpose(2, 3, 0, 1).reshape(81, 81)
+    line, u = lax.optimization_barrier((line, u))
     left, lower = line[:, 0], line[:, 1]
     left_right, left_left = from_x(left, 1), from_x(left, -1)
     lower_right, lower_left = from_x(lower, 1), from_x(lower, -1)
     left_far, lower_far = from_x(left_right, 1), from_x(lower_left, -1)
-    spread = mix(site, u, (left, left_right, left_far, left_left))
+    spread = mix(site_block, u, (left, left_right, left_far, left_left))
     lines = (lower, lower_right, lower_far, lower_left)
     theirs = contract_lower(1, spread, lines)
     ours = contract_lower(0, spread, lines)

time: 91.2 us -> 89.5 us (0.981)
  local copies, waits for them, and re-layouts: 1.74 us -> 0.04 us
    reshape x2 -> x0, local copies, waits for them, and re-layouts: 1.7 us -> none  [local(): site = site_block.transpose(2, 3, 0, 1).reshape(81, 81)]
  transfers between devices with their start and end apart: 8 -> 8, of which waited for: 3 -> 4; matrix products, arithmetic and copies ran while one was open for 2% -> 0% of each run, Pallas kernels for 6% -> 7%
where the time goes in v5:
time: 89.5 us; the launch traced here: 89 us
  blocking collectives  41.5 us (46%)
  starting transfers between devices  30.7 us (34%)
  Pallas kernels  11.8 us (13%)
  waiting for transfers between devices  4.77 us (5%)
    all_gather x1, blocking collectives, local(): u = lax.all_gather(u, 'lo', axis=0)  26.3 us
    ppermute x6, starting transfers between devices, from_x(): return lax.ppermute(value, 'up', pairs)  19 us
    all_to_all x1, blocking collectives, local(): terms = lax.all_to_all(terms, 'lo', 0, 0, axis_index_groups=Z_GROUPS)  15.2 us
    all_to_all x1, starting transfers between devices, local(): line = lax.all_to_all(lb, 'up', 0, 0, axis_index_groups=Y_GROUPS)  7.65 us
    ppermute x6, waiting for transfers between devices, from_x(): return lax.ppermute(value, 'up', pairs)  4.77 us
    pallas_call x1, Pallas kernels, mix(): pl.pallas_call(mix_kernel, out_shape=jax.ShapeDtypeStruct((SEC * 256, SEC...  4.42 us
    ppermute x1, starting transfers between devices, local(): theirs = lax.ppermute(theirs, 'lo', swap)  4.07 us
    pallas_call x2, Pallas kernels, contract_lower(): pl.pallas_call(functools.partial(lower_kernel, half), out_shape=jax.Shape...  3.66 us
  transfers between devices with their start and end apart: 8, of which 4 were waited for; matrix products, arithmetic and copies ran while one was open for 0% of the time, Pallas kernels for 7%

profile of v5, /device:TPU:1, one launch (start us, length us, event | category | flops | bytes accessed | tf_op | source)
XLA Modules:
  0.0 89.0 jit_solution(18373286680999034347)
XLA Ops:
  0.0 0.0 copy-start
  0.0 2.9 %prepare.1 = (bf16[8,2,144,128]{3,2,1,0:T(8,128)(2,1)}, bf16[192,128]{1,0:T(8,128)(2,1)}) custom-call(s32[8]{0:T(128)} %sizes.1, bf16[9,24,96]{2,1,0:T(8,128)(2,1)} %left.1, bf16[9,12,192]{2,1,0:T(8,128)(2,1)} %upper.1, bf16[9,12,192]{2,1,0:T(8,128)(2,1)} %lower.1), custom_call_target="tpu_custom_call" | custom-call | tf_op jit(solution)/shard_map/prepare/pallas_call | solution.py:130
  2.9 7.7 %all-to-all-start = ((bf16[8,2,144,128]{3,2,1,0:T(8,128)(2,1)}), bf16[8,2,144,128]{3,2,1,0:T(8,128)(2,1)S(1)}, u32[]{:S(2)}, u32[]{:S(2)}) async-start(bf16[8,2,144,128]{3,2,1,0:T(8,128)(2,1)} %get-tuple-element.9), calls=%async_computation | async-start | bytes 1179648 | tf_op jit(solution)/shard_map/all_to_all | solution.py:337
  10.5 26.3 %all-gather = bf16[3072,128]{1,0:T(8,128)(2,1)S(1)} all-gather(bf16[192,128]{1,0:T(8,128)(2,1)} %get-tuple-element.10), channel_id=2, replica_groups=mesh['up'=32,'lo'=16] {'lo'}, dimensions={0}, use_global_device_ids=true | all-gather | bytes 835584 | tf_op jit(solution)/shard_map/all_gather | solution.py:338
  36.9 0.0 all-to-all-done
  36.9 4.4 %collective-permute-start = (bf16[8,144,128]{2,1,0:T(8,128)(2,1)S(1)}, bf16[8,144,128]{2,1,0:T(8,128)(2,1)S(1)}, u32[]{:S(2)}, u32[]{:S(2)}) collective-permute-start(bf16[8,144,128]{2,1,0:T(8,128)(2,1)S(1)} %get-tuple-element.14.own), channel_id=1, source_target_pairs={{0,48},{16,0},{32,16},{48,32},{64,112},{80,64},{96,80},{112,96},{1... | collective-permute-start | bytes 884744 | tf_op jit(solution)/shard_map/ppermute | solution.py:332
  41.3 1.9 %collective-permute-start.4 = (bf16[8,144,128]{2,1,0:T(8,128)(2,1)S(1)}, bf16[8,144,128]{2,1,0:T(8,128)(2,1)S(1)}, u32[]{:S(2)}, u32[]{:S(2)}) collective-permute-start(bf16[8,144,128]{2,1,0:T(8,128)(2,1)S(1)} %get-tuple-element.13.own), channel_id=1, source_target_pairs={{0,16},{16,32},{32,48},{48,0},{64,80},{80,96},{96,112},{112,64},{1... | collective-permute-start | bytes 884744 | tf_op jit(solution)/shard_map/ppermute | solution.py:332
  43.2 2.1 %collective-permute-start.2 = (bf16[8,144,128]{2,1,0:T(8,128)(2,1)S(1)}, bf16[8,144,128]{2,1,0:T(8,128)(2,1)S(1)}, u32[]{:S(2)}, u32[]{:S(2)}) collective-permute-start(bf16[8,144,128]{2,1,0:T(8,128)(2,1)S(1)} %get-tuple-element.14.own), channel_id=1, source_target_pairs={{0,16},{16,32},{32,48},{48,0},{64,80},{80,96},{96,112},{112,64},{1... | collective-permute-start | bytes 884744 | tf_op jit(solution)/shard_map/ppermute | solution.py:332
  45.3 2.2 %collective-permute-done.right = bf16[8,144,128]{2,1,0:T(8,128)(2,1)S(1)} collective-permute-done((bf16[8,144,128]{2,1,0:T(8,128)(2,1)S(1)}, bf16[8,144,128]{2,1,0:T(8,128)(2,1)S(1)}, u32[]{:S(2)}, u32[]{:S(2)}) %collective-permute-start) | collective-permute-done | bytes 294944 | tf_op jit(solution)/shard_map/ppermute | solution.py:332
  47.5 5.3 %collective-permute-start.1 = (bf16[8,144,128]{2,1,0:T(8,128)(2,1)S(1)}, bf16[8,144,128]{2,1,0:T(8,128)(2,1)S(1)}, u32[]{:S(2)}, u32[]{:S(2)}) collective-permute-start(bf16[8,144,128]{2,1,0:T(8,128)(2,1)S(1)} %collective-permute-done.right), channel_id=1, source_target_pairs={{0,48},{16,0},{32,16},{48,32},{64,112},{80,64},{96,80},{112,96},{1... | collective-permute-start | bytes 884744 | tf_op jit(solution)/shard_map/ppermute | solution.py:332
  52.8 1.9 %collective-permute-start.3 = (bf16[8,144,128]{2,1,0:T(8,128)(2,1)S(1)}, bf16[8,144,128]{2,1,0:T(8,128)(2,1)S(1)}, u32[]{:S(2)}, u32[]{:S(2)}) collective-permute-start(bf16[8,144,128]{2,1,0:T(8,128)(2,1)S(1)} %get-tuple-element.13.own), channel_id=1, source_target_pairs={{0,48},{16,0},{32,16},{48,32},{64,112},{80,64},{96,80},{112,96},{1... | collective-permute-start | bytes 884744 | tf_op jit(solution)/shard_map/ppermute | solution.py:332
  54.8 0.0 collective-permute-done.4.left
  54.8 3.4 %collective-permute-start.5 = (bf16[8,144,128]{2,1,0:T(8,128)(2,1)S(1)}, bf16[8,144,128]{2,1,0:T(8,128)(2,1)S(1)}, u32[]{:S(2)}, u32[]{:S(2)}) collective-permute-start(bf16[8,144,128]{2,1,0:T(8,128)(2,1)S(1)} %collective-permute-done.4.left), channel_id=1, source_target_pairs={{0,16},{16,32},{32,48},{48,0},{64,80},{80,96},{96,112},{112,64},{1... | collective-permute-start | bytes 884744 | tf_op jit(solution)/shard_map/ppermute | solution.py:332
  58.2 0.7 collective-permute-done.2.left
  58.9 0.0 collective-permute-done.1.far
  58.9 0.0 copy-done
  58.9 4.4 %mix.1.spread = bf16[2048,768]{1,0:T(8,128)(2,1)S(1)} custom-call(f32[9,9,9,9]{3,2,1,0:T(8,128)S(1)} %copy-done, bf16[16,192,128]{2,1,0:T(8,128)(2,1)S(1)} %bitcast.5, bf16[8,144,128]{2,1,0:T(8,128)(2,1)S(1)} %get-tuple-element.14.own, bf16[8,144,128]{2,1,0:T(8,128)(2,1)S(1)} %collective-permute-done.right, ...), custom_call_target="tpu_custom_call" | custom-call | flops 6000000000 | bytes 3000000 | tf_op jit(solution)/shard_map/mix/pallas_call | solution.py:249
  63.3 1.2 %collective-permute-done.3.right = bf16[8,144,128]{2,1,0:T(8,128)(2,1)S(1)} collective-permute-done((bf16[8,144,128]{2,1,0:T(8,128)(2,1)S(1)}, bf16[8,144,128]{2,1,0:T(8,128)(2,1)S(1)}, u32[]{:S(2)}, u32[]{:S(2)}) %collective-permute-start.3) | collective-permute-done | bytes 294944 | tf_op jit(solution)/shard_map/ppermute | solution.py:332
  64.5 0.7 collective-permute-done.5.far
  65.1 1.8 %lower_theirs.1 = bf16[8,24,768]{2,1,0:T(8,128)(2,1)S(1)} custom-call(bf16[2048,768]{1,0:T(8,128)(2,1)S(1)} %mix.1.spread, bf16[8,144,128]{2,1,0:T(8,128)(2,1)S(1)} %get-tuple-element.13.own, bf16[8,144,128]{2,1,0:T(8,128)(2,1)S(1)} %collective-permute-done.3.right, bf16[8,144,128]{2,1,0:T(8,128)(2,1)S(1)} %collective-permute-done.5.far, ...), custom_call_target="tpu_custom_call" | custom-call | flops 3000000000 | bytes 3000000 | tf_op jit(solution)/shard_map/lower_theirs/pallas_call | solution.py:284
  67.0 4.1 %collective-permute-start.6 = (bf16[8,24,768]{2,1,0:T(8,128)(2,1)S(1)}, bf16[8,24,768]{2,1,0:T(8,128)(2,1)S(1)}, u32[]{:S(2)}, u32[]{:S(2)}) collective-permute-start(bf16[8,24,768]{2,1,0:T(8,128)(2,1)S(1)} %lower_theirs.1), channel_id=1, source_target_pairs={{0,1},{1,0},{2,3},{3,2},{4,5},{5,4},{6,7},{7,6},{8,9},{9,8},{10,11... | collective-permute-start | bytes 884744 | tf_op jit(solution)/shard_map/ppermute | solution.py:349
  71.1 1.8 %lower_ours.1 = f32[8,24,768]{2,1,0:T(8,128)S(1)} custom-call(bf16[2048,768]{1,0:T(8,128)(2,1)S(1)} %mix.1.spread, bf16[8,144,128]{2,1,0:T(8,128)(2,1)S(1)} %get-tuple-element.13.own, bf16[8,144,128]{2,1,0:T(8,128)(2,1)S(1)} %collective-permute-done.3.right, bf16[8,144,128]{2,1,0:T(8,128)(2,1)S(1)} %collective-permute-done.5.far, ...), custom_call_target="tpu_custom_call" | custom-call | flops 3000000000 | bytes 3000000 | tf_op jit(solution)/shard_map/lower_ours/pallas_call | solution.py:284
  72.9 0.0 collective-permute-done.6
  72.9 0.1 add_convert_fusion
  73.0 15.2 %all_to_all.10.terms = bf16[8,24,768]{2,1,0:T(8,128)(2,1)S(1)} all-to-all(bf16[8,24,768]{2,1,0:T(8,128)(2,1)S(1)} %add_convert_fusion), channel_id=1, replica_groups={{0,2,4,6,8,10,12,14},{1,3,5,7,9,11,13,15},{16,18,20,22,24,26,28,30},{17..., dimensions={0} | all-to-all | bytes 589824 | tf_op jit(solution)/shard_map/all_to_all | solution.py:351
  88.2 0.9 finish.1
  (1 shorter events, 0.0 us)
Async XLA Ops:
  0.0 58.9 %copy-start = (f32[9,9,9,9]{3,2,1,0:T(8,128)S(1)}, f32[9,9,9,9]{3,2,1,0:T(8,128)}, u32[]{:S(2)}) copy-start(f32[9,9,9,9]{3,2,1,0:T(8,128)} %site.1) | copy-start | bytes 78736
  2.9 34.0 %all-to-all-start = ((bf16[8,2,144,128]{3,2,1,0:T(8,128)(2,1)}), bf16[8,2,144,128]{3,2,1,0:T(8,128)(2,1)S(1)}, u32[]{:S(2)}, u32[]{:S(2)}) async-start(bf16[8,2,144,128]{3,2,1,0:T(8,128)(2,1)} %get-tuple-element.9), calls=%async_computation | async-start | bytes 1179648 | tf_op jit(solution)/shard_map/all_to_all | solution.py:337
  36.9 10.6 %collective-permute-start = (bf16[8,144,128]{2,1,0:T(8,128)(2,1)S(1)}, bf16[8,144,128]{2,1,0:T(8,128)(2,1)S(1)}, u32[]{:S(2)}, u32[]{:S(2)}) collective-permute-start(bf16[8,144,128]{2,1,0:T(8,128)(2,1)S(1)} %get-tuple-element.14.own), channel_id=1, source_target_pairs={{0,48},{16,0},{32,16},{48,32},{64,112},{80,64},{96,80},{112,96},{1... | collective-permute-start | bytes 884744 | tf_op jit(solution)/shard_map/ppermute | solution.py:332
  41.3 13.5 %collective-permute-start.4 = (bf16[8,144,128]{2,1,0:T(8,128)(2,1)S(1)}, bf16[8,144,128]{2,1,0:T(8,128)(2,1)S(1)}, u32[]{:S(2)}, u32[]{:S(2)}) collective-permute-start(bf16[8,144,128]{2,1,0:T(8,128)(2,1)S(1)} %get-tuple-element.13.own), channel_id=1, source_target_pairs={{0,16},{16,32},{32,48},{48,0},{64,80},{80,96},{96,112},{112,64},{1... | collective-permute-start | bytes 884744 | tf_op jit(solution)/shard_map/ppermute | solution.py:332
  43.2 15.6 %collective-permute-start.2 = (bf16[8,144,128]{2,1,0:T(8,128)(2,1)S(1)}, bf16[8,144,128]{2,1,0:T(8,128)(2,1)S(1)}, u32[]{:S(2)}, u32[]{:S(2)}) collective-permute-start(bf16[8,144,128]{2,1,0:T(8,128)(2,1)S(1)} %get-tuple-element.14.own), channel_id=1, source_target_pairs={{0,16},{16,32},{32,48},{48,0},{64,80},{80,96},{96,112},{112,64},{1... | collective-permute-start | bytes 884744 | tf_op jit(solution)/shard_map/ppermute | solution.py:332
  47.5 11.3 %collective-permute-start.1 = (bf16[8,144,128]{2,1,0:T(8,128)(2,1)S(1)}, bf16[8,144,128]{2,1,0:T(8,128)(2,1)S(1)}, u32[]{:S(2)}, u32[]{:S(2)}) collective-permute-start(bf16[8,144,128]{2,1,0:T(8,128)(2,1)S(1)} %collective-permute-done.right), channel_id=1, source_target_pairs={{0,48},{16,0},{32,16},{48,32},{64,112},{80,64},{96,80},{112,96},{1... | collective-permute-start | bytes 884744 | tf_op jit(solution)/shard_map/ppermute | solution.py:332
  52.8 11.6 %collective-permute-start.3 = (bf16[8,144,128]{2,1,0:T(8,128)(2,1)S(1)}, bf16[8,144,128]{2,1,0:T(8,128)(2,1)S(1)}, u32[]{:S(2)}, u32[]{:S(2)}) collective-permute-start(bf16[8,144,128]{2,1,0:T(8,128)(2,1)S(1)} %get-tuple-element.13.own), channel_id=1, source_target_pairs={{0,48},{16,0},{32,16},{48,32},{64,112},{80,64},{96,80},{112,96},{1... | collective-permute-start | bytes 884744 | tf_op jit(solution)/shard_map/ppermute | solution.py:332
  54.8 10.4 %collective-permute-start.5 = (bf16[8,144,128]{2,1,0:T(8,128)(2,1)S(1)}, bf16[8,144,128]{2,1,0:T(8,128)(2,1)S(1)}, u32[]{:S(2)}, u32[]{:S(2)}) collective-permute-start(bf16[8,144,128]{2,1,0:T(8,128)(2,1)S(1)} %collective-permute-done.4.left), channel_id=1, source_target_pairs={{0,16},{16,32},{32,48},{48,0},{64,80},{80,96},{96,112},{112,64},{1... | collective-permute-start | bytes 884744 | tf_op jit(solution)/shard_map/ppermute | solution.py:332
  67.0 5.9 %collective-permute-start.6 = (bf16[8,24,768]{2,1,0:T(8,128)(2,1)S(1)}, bf16[8,24,768]{2,1,0:T(8,128)(2,1)S(1)}, u32[]{:S(2)}, u32[]{:S(2)}) collective-permute-start(bf16[8,24,768]{2,1,0:T(8,128)(2,1)S(1)} %lower_theirs.1), channel_id=1, source_target_pairs={{0,1},{1,0},{2,3},{3,2},{4,5},{5,4},{6,7},{7,6},{8,9},{9,8},{10,11... | collective-permute-start | bytes 884744 | tf_op jit(solution)/shard_map/ppermute | solution.py:349

commit v6 on v5

--- a/solution.py
+++ b/solution.py
@@ -203,9 +203,10 @@
                     moved[part * 128 + p * XB:part * 128 + (p + 1) * XB, k * 128:(k + 1) * 128] = (
                         rows[:, part * 128:(part + 1) * 128]
                     )
+    legs[...] = jnp.zeros(legs.shape, F32)
     for n in range(DD * DD):
         legs[n * 16:n * 16 + DD, 0:DD] = site[n // DD, n % DD]
-    a, b = iota((81, DD * 128), 0), iota((81, DD * 128), 1)
+    a, b = iota((88, DD * 128), 0), iota((88, DD * 128), 1)
     pos = (b % 128) // 8
     s = jnp.where(pos == 4, ORDER[4], jnp.where(pos == 5, ORDER[5], pos))
     widen = one_hot((s + (b // 128) * DD == a) & (pos < DD))
@@ -215,7 +216,7 @@
     balance = charge_of(b // 128) - charge_of(s) - charge_of(l)
     wide = []
     for r in range(DD):
-        rows = tn(legs[pl.ds(r, DD * DD, stride=16), :].astype(BF), widen)[0:16]
+        rows = tn(legs[pl.ds(r, 88, stride=16), :].astype(BF), widen)[0:16]
         wide.append(jnp.where(balance == -CHARGE[r], rows, 0.0))
     a, b = iota((8, DD * 128), 0), iota((8, DD * 128), 1)
     same = (b % 8 == a) & (b % 128 < 72)
@@ -257,7 +258,7 @@
             pltpu.VMEM((3 * 128, DD * 128), F32),
             pltpu.VMEM((DD, 3, 8, SEC * 96), F32),
             pltpu.VMEM((256, SEC * 96), BF),
-            pltpu.VMEM((DD * DD * 16, 128), F32),
+            pltpu.VMEM((89 * 16, 128), F32),
         ],
         compiler_params=PARAMS,
         cost_estimate=pl.CostEstimate(flops=6_000_000_000, bytes_accessed=3_000_000, transcendentals=0),

time: 89.5 us -> 89.5 us (level)
  no operation moved by 1% of the time
where the time goes in v6:
time: 89.5 us; the launch traced here: 89 us
  blocking collectives  41.5 us (46%)
  starting transfers between devices  30.7 us (34%)
  Pallas kernels  11.9 us (13%)
  waiting for transfers between devices  4.72 us (5%)
    all_gather x1, blocking collectives, local(): u = lax.all_gather(u, 'lo', axis=0)  26.3 us
    ppermute x6, starting transfers between devices, from_x(): return lax.ppermute(value, 'up', pairs)  19 us
    all_to_all x1, blocking collectives, local(): terms = lax.all_to_all(terms, 'lo', 0, 0, axis_index_groups=Z_GROUPS)  15.2 us
    all_to_all x1, starting transfers between devices, local(): line = lax.all_to_all(lb, 'up', 0, 0, axis_index_groups=Y_GROUPS)  7.65 us
    ppermute x6, waiting for transfers between devices, from_x(): return lax.ppermute(value, 'up', pairs)  4.72 us
    pallas_call x1, Pallas kernels, mix(): pl.pallas_call(mix_kernel, out_shape=jax.ShapeDtypeStruct((SEC * 256, SEC...  4.47 us
    ppermute x1, starting transfers between devices, local(): theirs = lax.ppermute(theirs, 'lo', swap)  4.07 us
    pallas_call x2, Pallas kernels, contract_lower(): pl.pallas_call(functools.partial(lower_kernel, half), out_shape=jax.Shape...  3.66 us
  transfers between devices with their start and end apart: 8, of which 4 were waited for; matrix products, arithmetic and copies ran while one was open for 0% of the time, Pallas kernels for 7%

profile of v6, /device:TPU:1, one launch (start us, length us, event | category | flops | bytes accessed | tf_op | source)
XLA Modules:
  0.0 89.0 jit_solution(16358210572282145901)
XLA Ops:
  0.0 0.0 copy-start
  0.0 2.9 %prepare.1 = (bf16[8,2,144,128]{3,2,1,0:T(8,128)(2,1)}, bf16[192,128]{1,0:T(8,128)(2,1)}) custom-call(s32[8]{0:T(128)} %sizes.1, bf16[9,24,96]{2,1,0:T(8,128)(2,1)} %left.1, bf16[9,12,192]{2,1,0:T(8,128)(2,1)} %upper.1, bf16[9,12,192]{2,1,0:T(8,128)(2,1)} %lower.1), custom_call_target="tpu_custom_call" | custom-call | tf_op jit(solution)/shard_map/prepare/pallas_call | solution.py:130
  2.9 7.7 %all-to-all-start = ((bf16[8,2,144,128]{3,2,1,0:T(8,128)(2,1)}), bf16[8,2,144,128]{3,2,1,0:T(8,128)(2,1)S(1)}, u32[]{:S(2)}, u32[]{:S(2)}) async-start(bf16[8,2,144,128]{3,2,1,0:T(8,128)(2,1)} %get-tuple-element.9), calls=%async_computation | async-start | bytes 1179648 | tf_op jit(solution)/shard_map/all_to_all | solution.py:338
  10.5 26.3 %all-gather = bf16[3072,128]{1,0:T(8,128)(2,1)S(1)} all-gather(bf16[192,128]{1,0:T(8,128)(2,1)} %get-tuple-element.10), channel_id=2, replica_groups=mesh['up'=32,'lo'=16] {'lo'}, dimensions={0}, use_global_device_ids=true | all-gather | bytes 835584 | tf_op jit(solution)/shard_map/all_gather | solution.py:339
  36.9 0.0 all-to-all-done
  36.9 4.4 %collective-permute-start = (bf16[8,144,128]{2,1,0:T(8,128)(2,1)S(1)}, bf16[8,144,128]{2,1,0:T(8,128)(2,1)S(1)}, u32[]{:S(2)}, u32[]{:S(2)}) collective-permute-start(bf16[8,144,128]{2,1,0:T(8,128)(2,1)S(1)} %get-tuple-element.14.own), channel_id=1, source_target_pairs={{0,48},{16,0},{32,16},{48,32},{64,112},{80,64},{96,80},{112,96},{1... | collective-permute-start | bytes 884744 | tf_op jit(solution)/shard_map/ppermute | solution.py:333
  41.3 1.9 %collective-permute-start.4 = (bf16[8,144,128]{2,1,0:T(8,128)(2,1)S(1)}, bf16[8,144,128]{2,1,0:T(8,128)(2,1)S(1)}, u32[]{:S(2)}, u32[]{:S(2)}) collective-permute-start(bf16[8,144,128]{2,1,0:T(8,128)(2,1)S(1)} %get-tuple-element.13.own), channel_id=1, source_target_pairs={{0,16},{16,32},{32,48},{48,0},{64,80},{80,96},{96,112},{112,64},{1... | collective-permute-start | bytes 884744 | tf_op jit(solution)/shard_map/ppermute | solution.py:333
  43.2 2.1 %collective-permute-start.2 = (bf16[8,144,128]{2,1,0:T(8,128)(2,1)S(1)}, bf16[8,144,128]{2,1,0:T(8,128)(2,1)S(1)}, u32[]{:S(2)}, u32[]{:S(2)}) collective-permute-start(bf16[8,144,128]{2,1,0:T(8,128)(2,1)S(1)} %get-tuple-element.14.own), channel_id=1, source_target_pairs={{0,16},{16,32},{32,48},{48,0},{64,80},{80,96},{96,112},{112,64},{1... | collective-permute-start | bytes 884744 | tf_op jit(solution)/shard_map/ppermute | solution.py:333
  45.3 2.2 %collective-permute-done.right = bf16[8,144,128]{2,1,0:T(8,128)(2,1)S(1)} collective-permute-done((bf16[8,144,128]{2,1,0:T(8,128)(2,1)S(1)}, bf16[8,144,128]{2,1,0:T(8,128)(2,1)S(1)}, u32[]{:S(2)}, u32[]{:S(2)}) %collective-permute-start) | collective-permute-done | bytes 294944 | tf_op jit(solution)/shard_map/ppermute | solution.py:333
  47.5 5.3 %collective-permute-start.1 = (bf16[8,144,128]{2,1,0:T(8,128)(2,1)S(1)}, bf16[8,144,128]{2,1,0:T(8,128)(2,1)S(1)}, u32[]{:S(2)}, u32[]{:S(2)}) collective-permute-start(bf16[8,144,128]{2,1,0:T(8,128)(2,1)S(1)} %collective-permute-done.right), channel_id=1, source_target_pairs={{0,48},{16,0},{32,16},{48,32},{64,112},{80,64},{96,80},{112,96},{1... | collective-permute-start | bytes 884744 | tf_op jit(solution)/shard_map/ppermute | solution.py:333
  52.8 1.9 %collective-permute-start.3 = (bf16[8,144,128]{2,1,0:T(8,128)(2,1)S(1)}, bf16[8,144,128]{2,1,0:T(8,128)(2,1)S(1)}, u32[]{:S(2)}, u32[]{:S(2)}) collective-permute-start(bf16[8,144,128]{2,1,0:T(8,128)(2,1)S(1)} %get-tuple-element.13.own), channel_id=1, source_target_pairs={{0,48},{16,0},{32,16},{48,32},{64,112},{80,64},{96,80},{112,96},{1... | collective-permute-start | bytes 884744 | tf_op jit(solution)/shard_map/ppermute | solution.py:333
  54.8 0.0 collective-permute-done.4.left
  54.8 3.4 %collective-permute-start.5 = (bf16[8,144,128]{2,1,0:T(8,128)(2,1)S(1)}, bf16[8,144,128]{2,1,0:T(8,128)(2,1)S(1)}, u32[]{:S(2)}, u32[]{:S(2)}) collective-permute-start(bf16[8,144,128]{2,1,0:T(8,128)(2,1)S(1)} %collective-permute-done.4.left), channel_id=1, source_target_pairs={{0,16},{16,32},{32,48},{48,0},{64,80},{80,96},{96,112},{112,64},{1... | collective-permute-start | bytes 884744 | tf_op jit(solution)/shard_map/ppermute | solution.py:333
  58.2 0.7 collective-permute-done.2.left
  58.9 0.0 collective-permute-done.1.far
  58.9 0.0 copy-done
  58.9 4.5 %mix.1.spread = bf16[2048,768]{1,0:T(8,128)(2,1)S(1)} custom-call(f32[9,9,9,9]{3,2,1,0:T(8,128)S(1)} %copy-done, bf16[16,192,128]{2,1,0:T(8,128)(2,1)S(1)} %bitcast.5, bf16[8,144,128]{2,1,0:T(8,128)(2,1)S(1)} %get-tuple-element.14.own, bf16[8,144,128]{2,1,0:T(8,128)(2,1)S(1)} %collective-permute-done.right, ...), custom_call_target="tpu_custom_call" | custom-call | flops 6000000000 | bytes 3000000 | tf_op jit(solution)/shard_map/mix/pallas_call | solution.py:250
  63.3 1.1 %collective-permute-done.3.right = bf16[8,144,128]{2,1,0:T(8,128)(2,1)S(1)} collective-permute-done((bf16[8,144,128]{2,1,0:T(8,128)(2,1)S(1)}, bf16[8,144,128]{2,1,0:T(8,128)(2,1)S(1)}, u32[]{:S(2)}, u32[]{:S(2)}) %collective-permute-start.3) | collective-permute-done | bytes 294944 | tf_op jit(solution)/shard_map/ppermute | solution.py:333
  64.5 0.7 collective-permute-done.5.far
  65.1 1.8 %lower_theirs.1 = bf16[8,24,768]{2,1,0:T(8,128)(2,1)S(1)} custom-call(bf16[2048,768]{1,0:T(8,128)(2,1)S(1)} %mix.1.spread, bf16[8,144,128]{2,1,0:T(8,128)(2,1)S(1)} %get-tuple-element.13.own, bf16[8,144,128]{2,1,0:T(8,128)(2,1)S(1)} %collective-permute-done.3.right, bf16[8,144,128]{2,1,0:T(8,128)(2,1)S(1)} %collective-permute-done.5.far, ...), custom_call_target="tpu_custom_call" | custom-call | flops 3000000000 | bytes 3000000 | tf_op jit(solution)/shard_map/lower_theirs/pallas_call | solution.py:285
  67.0 4.1 %collective-permute-start.6 = (bf16[8,24,768]{2,1,0:T(8,128)(2,1)S(1)}, bf16[8,24,768]{2,1,0:T(8,128)(2,1)S(1)}, u32[]{:S(2)}, u32[]{:S(2)}) collective-permute-start(bf16[8,24,768]{2,1,0:T(8,128)(2,1)S(1)} %lower_theirs.1), channel_id=1, source_target_pairs={{0,1},{1,0},{2,3},{3,2},{4,5},{5,4},{6,7},{7,6},{8,9},{9,8},{10,11... | collective-permute-start | bytes 884744 | tf_op jit(solution)/shard_map/ppermute | solution.py:350
  71.1 1.8 %lower_ours.1 = f32[8,24,768]{2,1,0:T(8,128)S(1)} custom-call(bf16[2048,768]{1,0:T(8,128)(2,1)S(1)} %mix.1.spread, bf16[8,144,128]{2,1,0:T(8,128)(2,1)S(1)} %get-tuple-element.13.own, bf16[8,144,128]{2,1,0:T(8,128)(2,1)S(1)} %collective-permute-done.3.right, bf16[8,144,128]{2,1,0:T(8,128)(2,1)S(1)} %collective-permute-done.5.far, ...), custom_call_target="tpu_custom_call" | custom-call | flops 3000000000 | bytes 3000000 | tf_op jit(solution)/shard_map/lower_ours/pallas_call | solution.py:285
  72.9 0.0 collective-permute-done.6
  72.9 0.1 add_convert_fusion
  73.0 15.2 %all_to_all.10.terms = bf16[8,24,768]{2,1,0:T(8,128)(2,1)S(1)} all-to-all(bf16[8,24,768]{2,1,0:T(8,128)(2,1)S(1)} %add_convert_fusion), channel_id=1, replica_groups={{0,2,4,6,8,10,12,14},{1,3,5,7,9,11,13,15},{16,18,20,22,24,26,28,30},{17..., dimensions={0} | all-to-all | bytes 589824 | tf_op jit(solution)/shard_map/all_to_all | solution.py:352
  88.2 0.9 finish.1
  (1 shorter events, 0.0 us)
Async XLA Ops:
  0.0 58.9 %copy-start = (f32[9,9,9,9]{3,2,1,0:T(8,128)S(1)}, f32[9,9,9,9]{3,2,1,0:T(8,128)}, u32[]{:S(2)}) copy-start(f32[9,9,9,9]{3,2,1,0:T(8,128)} %site.1) | copy-start | bytes 78736
  2.9 34.0 %all-to-all-start = ((bf16[8,2,144,128]{3,2,1,0:T(8,128)(2,1)}), bf16[8,2,144,128]{3,2,1,0:T(8,128)(2,1)S(1)}, u32[]{:S(2)}, u32[]{:S(2)}) async-start(bf16[8,2,144,128]{3,2,1,0:T(8,128)(2,1)} %get-tuple-element.9), calls=%async_computation | async-start | bytes 1179648 | tf_op jit(solution)/shard_map/all_to_all | solution.py:338
  36.9 10.6 %collective-permute-start = (bf16[8,144,128]{2,1,0:T(8,128)(2,1)S(1)}, bf16[8,144,128]{2,1,0:T(8,128)(2,1)S(1)}, u32[]{:S(2)}, u32[]{:S(2)}) collective-permute-start(bf16[8,144,128]{2,1,0:T(8,128)(2,1)S(1)} %get-tuple-element.14.own), channel_id=1, source_target_pairs={{0,48},{16,0},{32,16},{48,32},{64,112},{80,64},{96,80},{112,96},{1... | collective-permute-start | bytes 884744 | tf_op jit(solution)/shard_map/ppermute | solution.py:333
  41.3 13.5 %collective-permute-start.4 = (bf16[8,144,128]{2,1,0:T(8,128)(2,1)S(1)}, bf16[8,144,128]{2,1,0:T(8,128)(2,1)S(1)}, u32[]{:S(2)}, u32[]{:S(2)}) collective-permute-start(bf16[8,144,128]{2,1,0:T(8,128)(2,1)S(1)} %get-tuple-element.13.own), channel_id=1, source_target_pairs={{0,16},{16,32},{32,48},{48,0},{64,80},{80,96},{96,112},{112,64},{1... | collective-permute-start | bytes 884744 | tf_op jit(solution)/shard_map/ppermute | solution.py:333
  43.2 15.6 %collective-permute-start.2 = (bf16[8,144,128]{2,1,0:T(8,128)(2,1)S(1)}, bf16[8,144,128]{2,1,0:T(8,128)(2,1)S(1)}, u32[]{:S(2)}, u32[]{:S(2)}) collective-permute-start(bf16[8,144,128]{2,1,0:T(8,128)(2,1)S(1)} %get-tuple-element.14.own), channel_id=1, source_target_pairs={{0,16},{16,32},{32,48},{48,0},{64,80},{80,96},{96,112},{112,64},{1... | collective-permute-start | bytes 884744 | tf_op jit(solution)/shard_map/ppermute | solution.py:333
  47.5 11.3 %collective-permute-start.1 = (bf16[8,144,128]{2,1,0:T(8,128)(2,1)S(1)}, bf16[8,144,128]{2,1,0:T(8,128)(2,1)S(1)}, u32[]{:S(2)}, u32[]{:S(2)}) collective-permute-start(bf16[8,144,128]{2,1,0:T(8,128)(2,1)S(1)} %collective-permute-done.right), channel_id=1, source_target_pairs={{0,48},{16,0},{32,16},{48,32},{64,112},{80,64},{96,80},{112,96},{1... | collective-permute-start | bytes 884744 | tf_op jit(solution)/shard_map/ppermute | solution.py:333
  52.8 11.6 %collective-permute-start.3 = (bf16[8,144,128]{2,1,0:T(8,128)(2,1)S(1)}, bf16[8,144,128]{2,1,0:T(8,128)(2,1)S(1)}, u32[]{:S(2)}, u32[]{:S(2)}) collective-permute-start(bf16[8,144,128]{2,1,0:T(8,128)(2,1)S(1)} %get-tuple-element.13.own), channel_id=1, source_target_pairs={{0,48},{16,0},{32,16},{48,32},{64,112},{80,64},{96,80},{112,96},{1... | collective-permute-start | bytes 884744 | tf_op jit(solution)/shard_map/ppermute | solution.py:333
  54.8 10.4 %collective-permute-start.5 = (bf16[8,144,128]{2,1,0:T(8,128)(2,1)S(1)}, bf16[8,144,128]{2,1,0:T(8,128)(2,1)S(1)}, u32[]{:S(2)}, u32[]{:S(2)}) collective-permute-start(bf16[8,144,128]{2,1,0:T(8,128)(2,1)S(1)} %collective-permute-done.4.left), channel_id=1, source_target_pairs={{0,16},{16,32},{32,48},{48,0},{64,80},{80,96},{96,112},{112,64},{1... | collective-permute-start | bytes 884744 | tf_op jit(solution)/shard_map/ppermute | solution.py:333
  67.0 5.9 %collective-permute-start.6 = (bf16[8,24,768]{2,1,0:T(8,128)(2,1)S(1)}, bf16[8,24,768]{2,1,0:T(8,128)(2,1)S(1)}, u32[]{:S(2)}, u32[]{:S(2)}) collective-permute-start(bf16[8,24,768]{2,1,0:T(8,128)(2,1)S(1)} %lower_theirs.1), channel_id=1, source_target_pairs={{0,1},{1,0},{2,3},{3,2},{4,5},{5,4},{6,7},{7,6},{8,9},{9,8},{10,11... | collective-permute-start | bytes 884744 | tf_op jit(solution)/shard_map/ppermute | solution.py:350

commit v7 on v6

--- a/solution.py
+++ b/solution.py
@@ -118,11 +118,13 @@
     for v, (host, at) in enumerate(OUT_PLACES):
         row = SEC * 96 + v * XB
         pack[1, host * XB:(host + 1) * XB, at * JB:(at + 1) * JB] = folded[row:row + XB, 0:JB]
+    near = pack[:, :, 0:128].astype(BF)
+    far = pack[:, :, 128:192].astype(BF)
+    rest = [jnp.concatenate([far[side, 0:48], far[side, 48:96]], axis=1) for side in range(2)]
     for n in range(NY):
         for side in range(2):
-            lb_out[n, side, 0:96, :] = pack[side, :, 0:128].astype(BF)
-            lb_out[n, side, 96:144, 0:64] = pack[side, 0:48, 128:192].astype(BF)
-            lb_out[n, side, 96:144, 64:128] = pack[side, 48:96, 128:192].astype(BF)
+            lb_out[n, side, 0:96, :] = near[side]
+            lb_out[n, side, 96:144, :] = rest[side]
     u_out[...] = edge
 
 

time: 89.5 us -> 89.4 us (level)
  no operation moved by 1% of the time
where the time goes in v7:
time: 89.4 us; the launch traced here: 89 us
  blocking collectives  41.5 us (46%)
  starting transfers between devices  30.7 us (34%)
  Pallas kernels  11.8 us (13%)
  waiting for transfers between devices  4.71 us (5%)
    all_gather x1, blocking collectives, local(): u = lax.all_gather(u, 'lo', axis=0)  26.3 us
    ppermute x6, starting transfers between devices, from_x(): return lax.ppermute(value, 'up', pairs)  19 us
    all_to_all x1, blocking collectives, local(): terms = lax.all_to_all(terms, 'lo', 0, 0, axis_index_groups=Z_GROUPS)  15.2 us
    all_to_all x1, starting transfers between devices, local(): line = lax.all_to_all(lb, 'up', 0, 0, axis_index_groups=Y_GROUPS)  7.65 us
    ppermute x6, waiting for transfers between devices, from_x(): return lax.ppermute(value, 'up', pairs)  4.7 us
    pallas_call x1, Pallas kernels, mix(): pl.pallas_call(mix_kernel, out_shape=jax.ShapeDtypeStruct((SEC * 256, SEC...  4.48 us
    ppermute x1, starting transfers between devices, local(): theirs = lax.ppermute(theirs, 'lo', swap)  4.07 us
    pallas_call x2, Pallas kernels, contract_lower(): pl.pallas_call(functools.partial(lower_kernel, half), out_shape=jax.Shape...  3.66 us
  transfers between devices with their start and end apart: 8, of which 4 were waited for; matrix products, arithmetic and copies ran while one was open for 0% of the time, Pallas kernels for 7%

profile of v7, /device:TPU:1, one launch (start us, length us, event | category | flops | bytes accessed | tf_op | source)
XLA Modules:
  0.0 89.0 jit_solution(7275269787543265028)
XLA Ops:
  0.0 0.0 copy-start
  0.0 2.8 %prepare.1 = (bf16[8,2,144,128]{3,2,1,0:T(8,128)(2,1)}, bf16[192,128]{1,0:T(8,128)(2,1)}) custom-call(s32[8]{0:T(128)} %sizes.1, bf16[9,24,96]{2,1,0:T(8,128)(2,1)} %left.1, bf16[9,12,192]{2,1,0:T(8,128)(2,1)} %upper.1, bf16[9,12,192]{2,1,0:T(8,128)(2,1)} %lower.1), custom_call_target="tpu_custom_call" | custom-call | tf_op jit(solution)/shard_map/prepare/pallas_call | solution.py:132
  2.8 7.7 %all-to-all-start = ((bf16[8,2,144,128]{3,2,1,0:T(8,128)(2,1)}), bf16[8,2,144,128]{3,2,1,0:T(8,128)(2,1)S(1)}, u32[]{:S(2)}, u32[]{:S(2)}) async-start(bf16[8,2,144,128]{3,2,1,0:T(8,128)(2,1)} %get-tuple-element.9), calls=%async_computation | async-start | bytes 1179648 | tf_op jit(solution)/shard_map/all_to_all | solution.py:340
  10.4 26.3 %all-gather = bf16[3072,128]{1,0:T(8,128)(2,1)S(1)} all-gather(bf16[192,128]{1,0:T(8,128)(2,1)} %get-tuple-element.10), channel_id=2, replica_groups=mesh['up'=32,'lo'=16] {'lo'}, dimensions={0}, use_global_device_ids=true | all-gather | bytes 835584 | tf_op jit(solution)/shard_map/all_gather | solution.py:341
  36.8 0.0 all-to-all-done
  36.8 4.4 %collective-permute-start = (bf16[8,144,128]{2,1,0:T(8,128)(2,1)S(1)}, bf16[8,144,128]{2,1,0:T(8,128)(2,1)S(1)}, u32[]{:S(2)}, u32[]{:S(2)}) collective-permute-start(bf16[8,144,128]{2,1,0:T(8,128)(2,1)S(1)} %get-tuple-element.14.own), channel_id=1, source_target_pairs={{0,48},{16,0},{32,16},{48,32},{64,112},{80,64},{96,80},{112,96},{1... | collective-permute-start | bytes 884744 | tf_op jit(solution)/shard_map/ppermute | solution.py:335
  41.2 1.9 %collective-permute-start.4 = (bf16[8,144,128]{2,1,0:T(8,128)(2,1)S(1)}, bf16[8,144,128]{2,1,0:T(8,128)(2,1)S(1)}, u32[]{:S(2)}, u32[]{:S(2)}) collective-permute-start(bf16[8,144,128]{2,1,0:T(8,128)(2,1)S(1)} %get-tuple-element.13.own), channel_id=1, source_target_pairs={{0,16},{16,32},{32,48},{48,0},{64,80},{80,96},{96,112},{112,64},{1... | collective-permute-start | bytes 884744 | tf_op jit(solution)/shard_map/ppermute | solution.py:335
  43.2 2.1 %collective-permute-start.2 = (bf16[8,144,128]{2,1,0:T(8,128)(2,1)S(1)}, bf16[8,144,128]{2,1,0:T(8,128)(2,1)S(1)}, u32[]{:S(2)}, u32[]{:S(2)}) collective-permute-start(bf16[8,144,128]{2,1,0:T(8,128)(2,1)S(1)} %get-tuple-element.14.own), channel_id=1, source_target_pairs={{0,16},{16,32},{32,48},{48,0},{64,80},{80,96},{96,112},{112,64},{1... | collective-permute-start | bytes 884744 | tf_op jit(solution)/shard_map/ppermute | solution.py:335
  45.3 2.2 %collective-permute-done.right = bf16[8,144,128]{2,1,0:T(8,128)(2,1)S(1)} collective-permute-done((bf16[8,144,128]{2,1,0:T(8,128)(2,1)S(1)}, bf16[8,144,128]{2,1,0:T(8,128)(2,1)S(1)}, u32[]{:S(2)}, u32[]{:S(2)}) %collective-permute-start) | collective-permute-done | bytes 294944 | tf_op jit(solution)/shard_map/ppermute | solution.py:335
  47.5 5.3 %collective-permute-start.1 = (bf16[8,144,128]{2,1,0:T(8,128)(2,1)S(1)}, bf16[8,144,128]{2,1,0:T(8,128)(2,1)S(1)}, u32[]{:S(2)}, u32[]{:S(2)}) collective-permute-start(bf16[8,144,128]{2,1,0:T(8,128)(2,1)S(1)} %collective-permute-done.right), channel_id=1, source_target_pairs={{0,48},{16,0},{32,16},{48,32},{64,112},{80,64},{96,80},{112,96},{1... | collective-permute-start | bytes 884744 | tf_op jit(solution)/shard_map/ppermute | solution.py:335
  52.8 1.9 %collective-permute-start.3 = (bf16[8,144,128]{2,1,0:T(8,128)(2,1)S(1)}, bf16[8,144,128]{2,1,0:T(8,128)(2,1)S(1)}, u32[]{:S(2)}, u32[]{:S(2)}) collective-permute-start(bf16[8,144,128]{2,1,0:T(8,128)(2,1)S(1)} %get-tuple-element.13.own), channel_id=1, source_target_pairs={{0,48},{16,0},{32,16},{48,32},{64,112},{80,64},{96,80},{112,96},{1... | collective-permute-start | bytes 884744 | tf_op jit(solution)/shard_map/ppermute | solution.py:335
  54.7 0.0 collective-permute-done.4.left
  54.7 3.4 %collective-permute-start.5 = (bf16[8,144,128]{2,1,0:T(8,128)(2,1)S(1)}, bf16[8,144,128]{2,1,0:T(8,128)(2,1)S(1)}, u32[]{:S(2)}, u32[]{:S(2)}) collective-permute-start(bf16[8,144,128]{2,1,0:T(8,128)(2,1)S(1)} %collective-permute-done.4.left), channel_id=1, source_target_pairs={{0,16},{16,32},{32,48},{48,0},{64,80},{80,96},{96,112},{112,64},{1... | collective-permute-start | bytes 884744 | tf_op jit(solution)/shard_map/ppermute | solution.py:335
  58.1 0.7 collective-permute-done.2.left
  58.8 0.0 collective-permute-done.1.far
  58.8 0.0 copy-done
  58.8 4.5 %mix.1.spread = bf16[2048,768]{1,0:T(8,128)(2,1)S(1)} custom-call(f32[9,9,9,9]{3,2,1,0:T(8,128)S(1)} %copy-done, bf16[16,192,128]{2,1,0:T(8,128)(2,1)S(1)} %bitcast.5, bf16[8,144,128]{2,1,0:T(8,128)(2,1)S(1)} %get-tuple-element.14.own, bf16[8,144,128]{2,1,0:T(8,128)(2,1)S(1)} %collective-permute-done.right, ...), custom_call_target="tpu_custom_call" | custom-call | flops 6000000000 | bytes 3000000 | tf_op jit(solution)/shard_map/mix/pallas_call | solution.py:252
  63.3 1.1 %collective-permute-done.3.right = bf16[8,144,128]{2,1,0:T(8,128)(2,1)S(1)} collective-permute-done((bf16[8,144,128]{2,1,0:T(8,128)(2,1)S(1)}, bf16[8,144,128]{2,1,0:T(8,128)(2,1)S(1)}, u32[]{:S(2)}, u32[]{:S(2)}) %collective-permute-start.3) | collective-permute-done | bytes 294944 | tf_op jit(solution)/shard_map/ppermute | solution.py:335
  64.4 0.7 collective-permute-done.5.far
  65.1 1.8 %lower_theirs.1 = bf16[8,24,768]{2,1,0:T(8,128)(2,1)S(1)} custom-call(bf16[2048,768]{1,0:T(8,128)(2,1)S(1)} %mix.1.spread, bf16[8,144,128]{2,1,0:T(8,128)(2,1)S(1)} %get-tuple-element.13.own, bf16[8,144,128]{2,1,0:T(8,128)(2,1)S(1)} %collective-permute-done.3.right, bf16[8,144,128]{2,1,0:T(8,128)(2,1)S(1)} %collective-permute-done.5.far, ...), custom_call_target="tpu_custom_call" | custom-call | flops 3000000000 | bytes 3000000 | tf_op jit(solution)/shard_map/lower_theirs/pallas_call | solution.py:287
  66.9 4.1 %collective-permute-start.6 = (bf16[8,24,768]{2,1,0:T(8,128)(2,1)S(1)}, bf16[8,24,768]{2,1,0:T(8,128)(2,1)S(1)}, u32[]{:S(2)}, u32[]{:S(2)}) collective-permute-start(bf16[8,24,768]{2,1,0:T(8,128)(2,1)S(1)} %lower_theirs.1), channel_id=1, source_target_pairs={{0,1},{1,0},{2,3},{3,2},{4,5},{5,4},{6,7},{7,6},{8,9},{9,8},{10,11... | collective-permute-start | bytes 884744 | tf_op jit(solution)/shard_map/ppermute | solution.py:352
  71.0 1.8 %lower_ours.1 = f32[8,24,768]{2,1,0:T(8,128)S(1)} custom-call(bf16[2048,768]{1,0:T(8,128)(2,1)S(1)} %mix.1.spread, bf16[8,144,128]{2,1,0:T(8,128)(2,1)S(1)} %get-tuple-element.13.own, bf16[8,144,128]{2,1,0:T(8,128)(2,1)S(1)} %collective-permute-done.3.right, bf16[8,144,128]{2,1,0:T(8,128)(2,1)S(1)} %collective-permute-done.5.far, ...), custom_call_target="tpu_custom_call" | custom-call | flops 3000000000 | bytes 3000000 | tf_op jit(solution)/shard_map/lower_ours/pallas_call | solution.py:287
  72.8 0.0 collective-permute-done.6
  72.8 0.1 add_convert_fusion
  72.9 15.2 %all_to_all.10.terms = bf16[8,24,768]{2,1,0:T(8,128)(2,1)S(1)} all-to-all(bf16[8,24,768]{2,1,0:T(8,128)(2,1)S(1)} %add_convert_fusion), channel_id=1, replica_groups={{0,2,4,6,8,10,12,14},{1,3,5,7,9,11,13,15},{16,18,20,22,24,26,28,30},{17..., dimensions={0} | all-to-all | bytes 589824 | tf_op jit(solution)/shard_map/all_to_all | solution.py:354
  88.1 0.9 finish.1
  (1 shorter events, 0.0 us)
Async XLA Ops:
  0.0 58.8 %copy-start = (f32[9,9,9,9]{3,2,1,0:T(8,128)S(1)}, f32[9,9,9,9]{3,2,1,0:T(8,128)}, u32[]{:S(2)}) copy-start(f32[9,9,9,9]{3,2,1,0:T(8,128)} %site.1) | copy-start | bytes 78736
  2.8 34.0 %all-to-all-start = ((bf16[8,2,144,128]{3,2,1,0:T(8,128)(2,1)}), bf16[8,2,144,128]{3,2,1,0:T(8,128)(2,1)S(1)}, u32[]{:S(2)}, u32[]{:S(2)}) async-start(bf16[8,2,144,128]{3,2,1,0:T(8,128)(2,1)} %get-tuple-element.9), calls=%async_computation | async-start | bytes 1179648 | tf_op jit(solution)/shard_map/all_to_all | solution.py:340
  36.8 10.6 %collective-permute-start = (bf16[8,144,128]{2,1,0:T(8,128)(2,1)S(1)}, bf16[8,144,128]{2,1,0:T(8,128)(2,1)S(1)}, u32[]{:S(2)}, u32[]{:S(2)}) collective-permute-start(bf16[8,144,128]{2,1,0:T(8,128)(2,1)S(1)} %get-tuple-element.14.own), channel_id=1, source_target_pairs={{0,48},{16,0},{32,16},{48,32},{64,112},{80,64},{96,80},{112,96},{1... | collective-permute-start | bytes 884744 | tf_op jit(solution)/shard_map/ppermute | solution.py:335
  41.2 13.5 %collective-permute-start.4 = (bf16[8,144,128]{2,1,0:T(8,128)(2,1)S(1)}, bf16[8,144,128]{2,1,0:T(8,128)(2,1)S(1)}, u32[]{:S(2)}, u32[]{:S(2)}) collective-permute-start(bf16[8,144,128]{2,1,0:T(8,128)(2,1)S(1)} %get-tuple-element.13.own), channel_id=1, source_target_pairs={{0,16},{16,32},{32,48},{48,0},{64,80},{80,96},{96,112},{112,64},{1... | collective-permute-start | bytes 884744 | tf_op jit(solution)/shard_map/ppermute | solution.py:335
  43.2 15.6 %collective-permute-start.2 = (bf16[8,144,128]{2,1,0:T(8,128)(2,1)S(1)}, bf16[8,144,128]{2,1,0:T(8,128)(2,1)S(1)}, u32[]{:S(2)}, u32[]{:S(2)}) collective-permute-start(bf16[8,144,128]{2,1,0:T(8,128)(2,1)S(1)} %get-tuple-element.14.own), channel_id=1, source_target_pairs={{0,16},{16,32},{32,48},{48,0},{64,80},{80,96},{96,112},{112,64},{1... | collective-permute-start | bytes 884744 | tf_op jit(solution)/shard_map/ppermute | solution.py:335
  47.5 11.3 %collective-permute-start.1 = (bf16[8,144,128]{2,1,0:T(8,128)(2,1)S(1)}, bf16[8,144,128]{2,1,0:T(8,128)(2,1)S(1)}, u32[]{:S(2)}, u32[]{:S(2)}) collective-permute-start(bf16[8,144,128]{2,1,0:T(8,128)(2,1)S(1)} %collective-permute-done.right), channel_id=1, source_target_pairs={{0,48},{16,0},{32,16},{48,32},{64,112},{80,64},{96,80},{112,96},{1... | collective-permute-start | bytes 884744 | tf_op jit(solution)/shard_map/ppermute | solution.py:335
  52.8 11.6 %collective-permute-start.3 = (bf16[8,144,128]{2,1,0:T(8,128)(2,1)S(1)}, bf16[8,144,128]{2,1,0:T(8,128)(2,1)S(1)}, u32[]{:S(2)}, u32[]{:S(2)}) collective-permute-start(bf16[8,144,128]{2,1,0:T(8,128)(2,1)S(1)} %get-tuple-element.13.own), channel_id=1, source_target_pairs={{0,48},{16,0},{32,16},{48,32},{64,112},{80,64},{96,80},{112,96},{1... | collective-permute-start | bytes 884744 | tf_op jit(solution)/shard_map/ppermute | solution.py:335
  54.7 10.4 %collective-permute-start.5 = (bf16[8,144,128]{2,1,0:T(8,128)(2,1)S(1)}, bf16[8,144,128]{2,1,0:T(8,128)(2,1)S(1)}, u32[]{:S(2)}, u32[]{:S(2)}) collective-permute-start(bf16[8,144,128]{2,1,0:T(8,128)(2,1)S(1)} %collective-permute-done.4.left), channel_id=1, source_target_pairs={{0,16},{16,32},{32,48},{48,0},{64,80},{80,96},{96,112},{112,64},{1... | collective-permute-start | bytes 884744 | tf_op jit(solution)/shard_map/ppermute | solution.py:335
  66.9 5.9 %collective-permute-start.6 = (bf16[8,24,768]{2,1,0:T(8,128)(2,1)S(1)}, bf16[8,24,768]{2,1,0:T(8,128)(2,1)S(1)}, u32[]{:S(2)}, u32[]{:S(2)}) collective-permute-start(bf16[8,24,768]{2,1,0:T(8,128)(2,1)S(1)} %lower_theirs.1), channel_id=1, source_target_pairs={{0,1},{1,0},{2,3},{3,2},{4,5},{5,4},{6,7},{7,6},{8,9},{9,8},{10,11... | collective-permute-start | bytes 884744 | tf_op jit(solution)/shard_map/ppermute | solution.py:352
